TPU v7x, 32 devices: a whole 2x2x4 slice. The times are simulated.
32 devices in a mesh: grp: 2 (over x), ep: 16 (over z, y, core).
Axes of the slice: x: 2, y: 2, z: 4, core: 2. Of those that a mesh axis runs over, the one named last changes fastest.
Arguments:
- states: bfloat16 [2, 1280, 2048], P(None, ('grp', 'ep')), may hold values from -6 to 6
- route_ids: int32 [2, 1280, 8], P(None, ('grp', 'ep')), may hold values from 0 to 15, all different within a row; in each aligned block of 40 rows (0 to 39, 40 to 79, ..., all dimensions but the last counted through in order) at most 30 rows name the same one
- route_gates: float32 [2, 1280, 8], P(None, ('grp', 'ep')), may hold values from 0.02 to 0.3
- moe_gain: float32 [2048], replicated, may hold values from 0.25 to 1.75
- final_gain: float32 [2048], replicated, may hold values from 0.25 to 1.75
- gate_proj: bfloat16 [16, 2048, 512], P('ep', 'grp'), may hold values from -0.125 to 0.125
- up_proj: bfloat16 [16, 2048, 512], P('ep', 'grp'), may hold values from -0.125 to 0.125
- down_proj: bfloat16 [16, 512, 2048], P('ep', 'grp'), may hold values from -0.25 to 0.25
- old_slots: int32 [16], replicated, may hold values from 0 to 15, each once
- new_slots: int32 [16], replicated, may hold values from 0 to 15, each once
- req_lengths: int32 [2, 2, 4], P(None, 'grp'), may hold values from 1 to 320, 640 in all within a row
- head_proj: bfloat16 [2048, 49152], P(None, ('grp', 'ep')), may hold values from -14 to 14
Outputs:
- mixed: bfloat16 [2, 1280, 2048], P(None, ('grp', 'ep'))
- moved_gate: bfloat16 [16, 2048, 512], P('ep', 'grp')
- moved_up: bfloat16 [16, 2048, 512], P('ep', 'grp')
- moved_down: bfloat16 [16, 512, 2048], P('ep', 'grp')
- log_probs: float32 [2, 8, 49152], P(None, None, ('grp', 'ep'))
Inputs may be any that keep to these rules, and one draw needn't show every extreme that they name: `route_ids`: in each aligned block of 40 rows (the rows of one device in one batch) no expert is named by more than 30 rows, a bound that some block reaches; the 8 ids of a row differ. `old_slots`: each expert once. `new_slots`: each expert once. `req_lengths`: the 4 lengths of a group in a batch sum to 640, and the largest is 320.
All inputs are finite; a program needn't handle non-finite values.
Results may differ from a plain program's by a relative error of at most 0.0035.
Values may be sent and summed in bfloat16 or wider, within the bound.
A program may use at most 128 MiB of HBM per device.

v0:
```python
import jax
import jax.numpy as jnp
from jax import lax
from jax.sharding import PartitionSpec as P


def normalize(rows, gain):
    scale = lax.rsqrt(jnp.mean(rows * rows, axis=-1, keepdims=True) + 1e-06)
    return (rows * scale * gain).astype(jnp.bfloat16)


def owner_table(placement):
    ident = jnp.arange(placement.shape[0], dtype=jnp.int32)
    hits = placement[None, :] == ident[:, None]
    return jnp.sum(jnp.where(hits, ident[None, :], 0), axis=1)


def reorder_blocks(weights, source, n_dest):
    shape = weights.shape
    blocks = weights.reshape(shape[0], shape[1], n_dest, shape[2] // n_dest)
    return jnp.take(blocks, source, axis=2).reshape(shape)


def build_sends(normed, expert_ids, owner, n_dest, capacity):
    tok_rows, top_count = expert_ids.shape
    experts_all = owner.shape[0]
    expert_hits = expert_ids[:, :, None] == jnp.arange(experts_all, dtype=jnp.int32)[None, None, :]
    destination = jnp.sum(jnp.where(expert_hits, owner[None, None, :], 0), axis=2)
    flat_dest = destination.reshape(-1)
    dest_hits = (flat_dest[:, None] == jnp.arange(n_dest, dtype=jnp.int32)[None, :]).astype(
        jnp.int32
    )
    earlier = jnp.cumsum(dest_hits, axis=0) - dest_hits
    position = jnp.sum(earlier * dest_hits, axis=1)
    slot_index = (flat_dest * capacity + position).reshape(tok_rows, top_count)
    slot_hits = (
        slot_index[:, :, None] == jnp.arange(n_dest * capacity, dtype=jnp.int32)[None, None, :]
    )
    selector = jnp.sum(slot_hits.astype(jnp.float32), axis=1).astype(jnp.bfloat16)
    sends = jnp.einsum("ts,td->sd", selector, normed, preferred_element_type=jnp.float32).astype(
        jnp.bfloat16
    )
    return (sends.reshape(n_dest, capacity, normed.shape[1]), slot_index)


def expert_block(rows, shards):
    gate_part, up_part, down_part = shards
    columns = rows
    gate_vals = jnp.dot(
        columns,
        lax.all_gather(gate_part, "grp", axis=1, tiled=True)[0],
        preferred_element_type=jnp.float32,
    )
    up_vals = jnp.dot(
        columns,
        lax.all_gather(up_part, "grp", axis=1, tiled=True)[0],
        preferred_element_type=jnp.float32,
    )
    hidden = (jax.nn.silu(gate_vals) * up_vals).astype(jnp.bfloat16)
    columns = hidden
    outputs = jnp.dot(
        columns,
        lax.all_gather(down_part, "grp", axis=1, tiled=True)[0],
        preferred_element_type=jnp.float32,
    )
    return outputs.astype(jnp.bfloat16)


def combine_rows(residual_rows, gates, returned_rows, slot_index):
    picked = returned_rows[slot_index].astype(jnp.float32)
    return (residual_rows + jnp.sum(gates[:, :, None] * picked, axis=1)).astype(jnp.bfloat16)


def per_device(
    states,
    route_ids,
    route_gates,
    moe_gain,
    final_gain,
    gate_proj,
    up_proj,
    down_proj,
    old_slots,
    new_slots,
    req_lengths,
    head_proj,
):
    n_dest = lax.axis_size("ep")
    column = lax.axis_index("ep")
    tok_rows = states.shape[1]
    width = states.shape[2]
    top_count = route_ids.shape[2]
    experts_all = old_slots.shape[0]
    capacity = min(tok_rows, max(2, 3 * tok_rows * top_count // (2 * experts_all)))
    old_owner = owner_table(old_slots)
    new_owner = owner_table(new_slots)
    source = jnp.take(old_owner, new_slots)
    spread = (
        lax.all_to_all(gate_proj, "ep", split_axis=2, concat_axis=2, tiled=True),
        lax.all_to_all(up_proj, "ep", split_axis=2, concat_axis=2, tiled=True),
        lax.all_to_all(down_proj, "ep", split_axis=2, concat_axis=2, tiled=True),
    )
    gate_sorted = reorder_blocks(spread[0], source, n_dest)
    up_sorted = reorder_blocks(spread[1], source, n_dest)
    down_sorted = reorder_blocks(spread[2], source, n_dest)
    moved = (
        lax.all_to_all(gate_sorted, "ep", split_axis=2, concat_axis=2, tiled=True),
        lax.all_to_all(up_sorted, "ep", split_axis=2, concat_axis=2, tiled=True),
        lax.all_to_all(down_sorted, "ep", split_axis=2, concat_axis=2, tiled=True),
    )
    moved_gate, moved_up, moved_down = moved
    residual = states.astype(jnp.float32)
    normed = normalize(residual, moe_gain)
    outputs = []
    for batch_index, owner, shards in (
        (0, old_owner, (gate_proj, up_proj, down_proj)),
        (1, new_owner, (moved_gate, moved_up, moved_down)),
    ):
        sends, slot_index = build_sends(
            normed[batch_index], route_ids[batch_index], owner, n_dest, capacity
        )
        arrived = lax.all_to_all(sends, "ep", split_axis=0, concat_axis=0, tiled=True)
        results = expert_block(arrived.reshape(n_dest * capacity, width), shards)
        returned = lax.all_to_all(
            results.reshape(n_dest, capacity, width), "ep", split_axis=0, concat_axis=0, tiled=True
        )
        outputs.append(
            combine_rows(
                residual[batch_index],
                route_gates[batch_index],
                returned.reshape(n_dest * capacity, width),
                slot_index,
            )
        )
    mixed = jnp.stack(outputs)
    request_ends = jnp.cumsum(req_lengths[:, 0, :], axis=-1) - 1
    local_ends = request_ends - column * tok_rows
    picker = (
        local_ends[:, :, None] == jnp.arange(tok_rows, dtype=jnp.int32)[None, None, :]
    ).astype(jnp.bfloat16)
    tail_terms = jnp.einsum("brt,btd->brd", picker, mixed, preferred_element_type=jnp.float32)
    group_tails = lax.psum(tail_terms.astype(jnp.bfloat16), "ep")
    gathered = lax.all_gather(group_tails, "grp", axis=1, tiled=True)
    finals = normalize(gathered.astype(jnp.float32), final_gain)
    logits = jnp.dot(finals.reshape(-1, width), head_proj, preferred_element_type=jnp.float32)
    top_val = lax.pmax(jnp.max(logits, axis=1), ("grp", "ep"))
    totals = lax.psum(jnp.sum(jnp.exp(logits - top_val[:, None]), axis=1), ("grp", "ep"))
    log_probs = (logits - top_val[:, None] - jnp.log(totals)[:, None]).reshape(
        2, -1, logits.shape[1]
    )
    return (mixed, moved_gate, moved_up, moved_down, log_probs)


def solution(mesh):
    placed = (
        P(None, ("grp", "ep"), None),
        P(None, ("grp", "ep"), None),
        P(None, ("grp", "ep"), None),
        P(),
        P(),
        P("ep", "grp", None),
        P("ep", "grp", None),
        P("ep", "grp", None),
        P(),
        P(),
        P(None, "grp", None),
        P(None, ("grp", "ep")),
    )
    return jax.shard_map(
        per_device,
        mesh=mesh,
        in_specs=placed,
        out_specs=(
            P(None, ("grp", "ep"), None),
            P("ep", "grp", None),
            P("ep", "grp", None),
            P("ep", "grp", None),
            P(None, None, ("grp", "ep")),
        ),
        check_vma=False,
    )
```

profile of v0, /device:TPU:0, one launch (start us, length us, event | category | flops | bytes accessed | tf_op | source)
XLA Modules:
  0.0 611.8 jit_solution(1638913436100575654)
XLA Ops:
  12.4 7.8 %reduce.6 = bf16[512,1024]{1,0:T(8,128)(2,1)} reduce(bf16[512,1,1024]{2,1,0:T(2,128)(2,1)S(1)} %bitcast.152, bf16[]{:T(256)} %broadcast.285), dimensions={1}, to_apply=%bitcast.118.reduce_sub_computation | reduce | bytes 2097154
  22.9 7.7 %all-to-all-start.3 = ((bf16[16,2,16384]{2,1,0:T(2,128)(2,1)}), bf16[16,2,16384]{2,1,0:T(2,128)(2,1)}, u32[]{:S(2)}, u32[]{:S(2)}) async-start(bf16[16,2,16384]{2,1,0:T(2,128)(2,1)} %reshape.355), calls=%async_computation.3 | async-start | bytes 2097152 | tf_op jit(solution)/shard_map/all_to_all | solution.py:99
  32.6 7.8 %reduce.7 = bf16[512,1024]{1,0:T(8,128)(2,1)} reduce(bf16[512,1,1024]{2,1,0:T(2,128)(2,1)S(1)} %bitcast.156, bf16[]{:T(256)} %broadcast.285), dimensions={1}, to_apply=%bitcast.114.reduce_sub_computation | reduce | bytes 2097154
  43.0 10.5 %all-to-all-done.3 = bf16[16,2,16384]{2,1,0:T(2,128)(2,1)} async-done(((bf16[16,2,16384]{2,1,0:T(2,128)(2,1)}), bf16[16,2,16384]{2,1,0:T(2,128)(2,1)}, u32[]{:S(2)}, u32[]{:S(2)}) %all-to-all-start.3) | async-done | bytes 1048608 | tf_op jit(solution)/shard_map/all_to_all | solution.py:99
  53.5 6.9 %all-to-all-start.5 = ((bf16[16,2,16384]{2,1,0:T(2,128)(2,1)}), bf16[16,2,16384]{2,1,0:T(2,128)(2,1)}, u32[]{:S(2)}, u32[]{:S(2)}) async-start(bf16[16,2,16384]{2,1,0:T(2,128)(2,1)} %reshape.351), calls=%async_computation.5 | async-start | bytes 2097152 | tf_op jit(solution)/shard_map/all_to_all | solution.py:100
  62.7 10.6 %reduce.4 = bf16[2048,256]{1,0:T(8,128)(2,1)S(1)} reduce(bf16[2048,1,256]{2,1,0:T(2,128)(2,1)S(1)} %bitcast.157, bf16[]{:T(256)} %broadcast.285), dimensions={1}, to_apply=%bitcast.110.reduce_sub_computation | reduce | bytes 2097154
  74.4 9.0 %all-to-all-done.5 = bf16[16,2,16384]{2,1,0:T(2,128)(2,1)} async-done(((bf16[16,2,16384]{2,1,0:T(2,128)(2,1)}), bf16[16,2,16384]{2,1,0:T(2,128)(2,1)}, u32[]{:S(2)}, u32[]{:S(2)}) %all-to-all-start.5) | async-done | bytes 1048608 | tf_op jit(solution)/shard_map/all_to_all | solution.py:100
  83.5 7.3 %all-to-all-start.7 = ((bf16[16,2,16384]{2,1,0:T(2,128)(2,1)}), bf16[16,2,16384]{2,1,0:T(2,128)(2,1)S(1)}, u32[]{:S(2)}, u32[]{:S(2)}) async-start(bf16[16,2,16384]{2,1,0:T(2,128)(2,1)} %reshape.347), calls=%async_computation.7 | async-start | bytes 2097152 | tf_op jit(solution)/shard_map/all_to_all | solution.py:101
  95.9 17.7 %all-to-all-done.7 = bf16[16,2,16384]{2,1,0:T(2,128)(2,1)S(1)} async-done(((bf16[16,2,16384]{2,1,0:T(2,128)(2,1)}), bf16[16,2,16384]{2,1,0:T(2,128)(2,1)S(1)}, u32[]{:S(2)}, u32[]{:S(2)}) %all-to-all-start.7) | async-done | bytes 1048608 | tf_op jit(solution)/shard_map/all_to_all | solution.py:101
  114.6 6.9 %all-to-all-start.2 = ((bf16[16,30,2048]{2,1,0:T(8,128)(2,1)}), bf16[16,30,2048]{2,1,0:T(8,128)(2,1)S(1)}, u32[]{:S(2)}, u32[]{:S(2)}) async-start(bf16[16,30,2048]{2,1,0:T(8,128)(2,1)} %reshape.258), calls=%async_computation.2 | async-start | bytes 4194304 | tf_op jit(solution)/shard_map/all_to_all | solution.py:122
  129.2 33.4 %all-to-all-done.2 = bf16[16,30,2048]{2,1,0:T(8,128)(2,1)S(1)} async-done(((bf16[16,30,2048]{2,1,0:T(8,128)(2,1)}), bf16[16,30,2048]{2,1,0:T(8,128)(2,1)S(1)}, u32[]{:S(2)}, u32[]{:S(2)}) %all-to-all-start.2) | async-done | bytes 1966112 | tf_op jit(solution)/shard_map/all_to_all | solution.py:122
  164.0 11.3 %all-to-all-start = ((bf16[16,30,2048]{2,1,0:T(8,128)(2,1)}), bf16[16,30,2048]{2,1,0:T(8,128)(2,1)}, u32[]{:S(2)}, u32[]{:S(2)}) async-start(bf16[16,30,2048]{2,1,0:T(8,128)(2,1)} %reshape.252), calls=%async_computation | async-start | bytes 4194304 | tf_op jit(solution)/shard_map/all_to_all | solution.py:122
  182.1 5.9 reshape.352
  193.2 7.8 %reduce.9 = bf16[512,1024]{1,0:T(8,128)(2,1)} reduce(bf16[512,1,1024]{2,1,0:T(2,128)(2,1)S(1)} %bitcast.154, bf16[]{:T(256)} %broadcast.285), dimensions={1}, to_apply=%bitcast.141.reduce_sub_computation | reduce | bytes 2097154
  203.6 12.8 %all-to-all-done = bf16[16,30,2048]{2,1,0:T(8,128)(2,1)} async-done(((bf16[16,30,2048]{2,1,0:T(8,128)(2,1)}), bf16[16,30,2048]{2,1,0:T(8,128)(2,1)}, u32[]{:S(2)}, u32[]{:S(2)}) %all-to-all-start) | async-done | bytes 1966112 | tf_op jit(solution)/shard_map/all_to_all | solution.py:122
  216.4 11.3 %all-to-all-start.4 = ((bf16[16,2,16384]{2,1,0:T(2,128)(2,1)}), bf16[16,2,16384]{2,1,0:T(2,128)(2,1)}, u32[]{:S(2)}, u32[]{:S(2)}) async-start(bf16[16,2,16384]{2,1,0:T(2,128)(2,1)} %reshape.357), calls=%async_computation.4 | async-start | bytes 2097152 | tf_op jit(solution)/shard_map/all_to_all | solution.py:107
  230.0 6.8 %reduce.8 = bf16[512,1024]{1,0:T(8,128)(2,1)S(1)} reduce(bf16[512,1,1024]{2,1,0:T(2,128)(2,1)S(1)} %bitcast.155, bf16[]{:T(256)} %broadcast.285), dimensions={1}, to_apply=%bitcast.140.reduce_sub_computation | reduce | bytes 2097154
  238.4 12.2 %all-to-all-done.4 = bf16[16,2,16384]{2,1,0:T(2,128)(2,1)} async-done(((bf16[16,2,16384]{2,1,0:T(2,128)(2,1)}), bf16[16,2,16384]{2,1,0:T(2,128)(2,1)}, u32[]{:S(2)}, u32[]{:S(2)}) %all-to-all-start.4) | async-done | bytes 1048608 | tf_op jit(solution)/shard_map/all_to_all | solution.py:107
  250.7 6.9 %all-to-all-start.6 = ((bf16[16,2,16384]{2,1,0:T(2,128)(2,1)}), bf16[16,2,16384]{2,1,0:T(2,128)(2,1)}, u32[]{:S(2)}, u32[]{:S(2)}) async-start(bf16[16,2,16384]{2,1,0:T(2,128)(2,1)} %reshape.353), calls=%async_computation.6 | async-start | bytes 2097152 | tf_op jit(solution)/shard_map/all_to_all | solution.py:108
  270.3 11.7 %copy.146 = bf16[1,256,2048]{1,0,2:T(2,128)(2,1)S(1)} copy(bf16[1,256,2048]{1,2,0:T(8,128)(2,1)S(1)} %bitcast_select_fusion.2) | data formatting | bytes 2097152 | tf_op jit(solution)/shard_map/jit(_take)/select_n | solution.py:21
  282.0 10.6 %reduce.5 = bf16[2048,256]{1,0:T(8,128)(2,1)S(1)} reduce(bf16[2048,1,256]{2,1,0:T(2,128)(2,1)S(1)} %bitcast.153, bf16[]{:T(256)} %broadcast.285), dimensions={1}, to_apply=%bitcast.139.reduce_sub_computation | reduce | bytes 2097154
  293.7 6.0 all-to-all-start.8
  313.9 6.1 convolution_convert_fusion.2
  322.8 6.7 %all-to-all-start.1 = ((bf16[16,30,2048]{2,1,0:T(8,128)(2,1)}), bf16[16,30,2048]{2,1,0:T(8,128)(2,1)}, u32[]{:S(2)}, u32[]{:S(2)}) async-start(bf16[16,30,2048]{2,1,0:T(8,128)(2,1)} %reshape.254), calls=%async_computation.1 | async-start | bytes 4194304 | tf_op jit(solution)/shard_map/all_to_all | solution.py:124
  339.8 11.9 %all-gather.15.cloned.1.call-done = bf16[1,2048,512]{2,1,0:T(8,128)(2,1)} async-done(((bf16[1,1024,512]{2,1,0:T(8,128)(2,1)}), bf16[1,2048,512]{2,1,0:T(8,128)(2,1)}) %all-gather.15.cloned.1.call-update) | async-done | bytes 2097168 | tf_op jit(solution)/shard_map/all_gather | solution.py:56
  351.7 35.1 %all-gather.17.cloned.1.call-done = bf16[1,512,2048]{2,1,0:T(8,128)(2,1)} async-done(((bf16[1,256,2048]{2,1,0:T(8,128)(2,1)}), bf16[1,512,2048]{2,1,0:T(8,128)(2,1)}) %all-gather.17.cloned.1.call-update) | async-done | bytes 2097168 | tf_op jit(solution)/shard_map/all_gather | solution.py:63
  386.8 5.9 convolution_convert_fusion
  395.5 5.8 all-to-all-start.9
  409.5 32.9 %all-to-all-done.9 = bf16[16,30,2048]{2,1,0:T(8,128)(2,1)} async-done(((bf16[16,30,2048]{2,1,0:T(8,128)(2,1)}), bf16[16,30,2048]{2,1,0:T(8,128)(2,1)}, u32[]{:S(2)}, u32[]{:S(2)}) %all-to-all-start.9) | async-done | bytes 1966112 | tf_op jit(solution)/shard_map/all_to_all | solution.py:124
  449.4 67.3 %psum.14 = bf16[2,4,2048]{2,1,0:T(4,128)(2,1)S(1)} all-reduce(bf16[2,4,2048]{2,1,0:T(4,128)(2,1)S(1)} %convolution_convert_fusion.4), channel_id=1, replica_groups=mesh['grp'=2,'ep'=16] {'ep'}, use_global_device_ids=true, to_apply=%region_16.18 | all-reduce | flops 16384 | bytes 65536 | tf_op jit(solution)/shard_map/psum | solution.py:142
  525.3 36.9 %pmax.7 = f32[16]{0:T(128)S(1)} all-reduce(f32[16]{0:T(128)S(1)} %get-tuple-element.41), channel_id=1, replica_groups=mesh['grp'=2,'ep'=16] {'grp','ep'}, use_global_device_ids=true, to_apply=%region_19.21 | all-reduce | flops 16 | bytes 128 | tf_op jit(solution)/shard_map/pmax | solution.py:146
  562.4 41.4 %psum.15 = f32[16]{0:T(128)S(1)} all-reduce(f32[16]{0:T(128)S(1)} %exponential_reduce_fusion), channel_id=1, replica_groups=mesh['grp'=2,'ep'=16] {'grp','ep'}, use_global_device_ids=true, to_apply=%region_21.23 | all-reduce | flops 16 | bytes 128 | tf_op jit(solution)/shard_map/psum | solution.py:147
  (167 shorter events, 117.8 us)
Async XLA Ops:
  20.2 10.4 %copy-start.2 = (bf16[1,1024,512]{2,1,0:T(8,128)(2,1)S(1)}, bf16[1,1024,512]{2,1,0:T(8,128)(2,1)}, u32[]{:S(2)}) copy-start(bf16[1,1024,512]{2,1,0:T(8,128)(2,1)} %param.20) | copy-start | bytes 3145732
  22.9 30.6 %all-to-all-start.3 = ((bf16[16,2,16384]{2,1,0:T(2,128)(2,1)}), bf16[16,2,16384]{2,1,0:T(2,128)(2,1)}, u32[]{:S(2)}, u32[]{:S(2)}) async-start(bf16[16,2,16384]{2,1,0:T(2,128)(2,1)} %reshape.355), calls=%async_computation.3 | async-start | bytes 2097152 | tf_op jit(solution)/shard_map/all_to_all | solution.py:99
  40.3 20.1 %copy-start.15 = (s32[16]{0:T(128)S(1)}, s32[16]{0:T(128)}, u32[]{:S(2)}) copy-start(s32[16]{0:T(128)} %param.22) | copy-start | bytes 196
  40.3 20.3 %copy-start.14 = (s32[16]{0:T(128)S(1)}, s32[16]{0:T(128)}, u32[]{:S(2)}) copy-start(s32[16]{0:T(128)} %param.23) | copy-start | bytes 196
  40.3 20.4 %copy-start.10 = (s32[2,40,8]{1,2,0:T(8,128)S(1)}, s32[2,40,8]{1,2,0:T(8,128)}, u32[]{:S(2)}) copy-start(s32[2,40,8]{1,2,0:T(8,128)} %param.15) | copy-start | bytes 7684
  40.3 20.7 %copy-start.1 = (bf16[1,256,2048]{2,1,0:T(8,128)(2,1)S(1)}, bf16[1,256,2048]{2,1,0:T(8,128)(2,1)}, u32[]{:S(2)}) copy-start(bf16[1,256,2048]{2,1,0:T(8,128)(2,1)} %param.21) | copy-start | bytes 3145732
  53.5 29.9 %all-to-all-start.5 = ((bf16[16,2,16384]{2,1,0:T(2,128)(2,1)}), bf16[16,2,16384]{2,1,0:T(2,128)(2,1)}, u32[]{:S(2)}, u32[]{:S(2)}) async-start(bf16[16,2,16384]{2,1,0:T(2,128)(2,1)} %reshape.351), calls=%async_computation.5 | async-start | bytes 2097152 | tf_op jit(solution)/shard_map/all_to_all | solution.py:100
  73.3 19.2 %copy-start.5 = (bf16[2,40,2048]{2,1,0:T(8,128)(2,1)S(1)}, bf16[2,40,2048]{2,1,0:T(8,128)(2,1)}, u32[]{:S(2)}) copy-start(bf16[2,40,2048]{2,1,0:T(8,128)(2,1)} %param.14) | copy-start | bytes 983044
  73.3 19.4 %copy-start.12 = (f32[2048]{0:T(1024)S(1)}, f32[2048]{0:T(1024)}, u32[]{:S(2)}) copy-start(f32[2048]{0:T(1024)} %param.17) | copy-start | bytes 24580
  83.5 30.2 %all-to-all-start.7 = ((bf16[16,2,16384]{2,1,0:T(2,128)(2,1)}), bf16[16,2,16384]{2,1,0:T(2,128)(2,1)S(1)}, u32[]{:S(2)}, u32[]{:S(2)}) async-start(bf16[16,2,16384]{2,1,0:T(2,128)(2,1)} %reshape.347), calls=%async_computation.7 | async-start | bytes 2097152 | tf_op jit(solution)/shard_map/all_to_all | solution.py:101
  92.8 0.7 copy-start.7
  113.6 1.0 copy-start.3
  114.6 48.0 %all-to-all-start.2 = ((bf16[16,30,2048]{2,1,0:T(8,128)(2,1)}), bf16[16,30,2048]{2,1,0:T(8,128)(2,1)S(1)}, u32[]{:S(2)}, u32[]{:S(2)}) async-start(bf16[16,30,2048]{2,1,0:T(8,128)(2,1)} %reshape.258), calls=%async_computation.2 | async-start | bytes 4194304 | tf_op jit(solution)/shard_map/all_to_all | solution.py:122
  162.6 1.4 copy-start
  164.0 52.4 %all-to-all-start = ((bf16[16,30,2048]{2,1,0:T(8,128)(2,1)}), bf16[16,30,2048]{2,1,0:T(8,128)(2,1)}, u32[]{:S(2)}, u32[]{:S(2)}) async-start(bf16[16,30,2048]{2,1,0:T(8,128)(2,1)} %reshape.252), calls=%async_computation | async-start | bytes 4194304 | tf_op jit(solution)/shard_map/all_to_all | solution.py:122
  175.2 134.9 %all-gather.7.cloned.1.call-start = ((), (), s32[]{:S(2)}) async-start(), calls=%async_computation.10 | async-start | bytes 3145728 | tf_op jit(solution)/shard_map/all_gather | solution.py:51
  176.0 137.9 %all-gather.11.cloned.1.call-start = ((), (), s32[]{:S(2)}) async-start(), calls=%async_computation.12 | async-start | bytes 3145728 | tf_op jit(solution)/shard_map/all_gather | solution.py:63
  216.4 34.3 %all-to-all-start.4 = ((bf16[16,2,16384]{2,1,0:T(2,128)(2,1)}), bf16[16,2,16384]{2,1,0:T(2,128)(2,1)}, u32[]{:S(2)}, u32[]{:S(2)}) async-start(bf16[16,2,16384]{2,1,0:T(2,128)(2,1)} %reshape.357), calls=%async_computation.4 | async-start | bytes 2097152 | tf_op jit(solution)/shard_map/all_to_all | solution.py:107
  227.7 86.2 %all-gather.9.cloned.1.call-start = ((), (), s32[]{:S(2)}) async-start(), calls=%async_computation.11 | async-start | bytes 3145728 | tf_op jit(solution)/shard_map/all_gather | solution.py:56
  250.7 43.1 %all-to-all-start.6 = ((bf16[16,2,16384]{2,1,0:T(2,128)(2,1)}), bf16[16,2,16384]{2,1,0:T(2,128)(2,1)}, u32[]{:S(2)}, u32[]{:S(2)}) async-start(bf16[16,2,16384]{2,1,0:T(2,128)(2,1)} %reshape.353), calls=%async_computation.6 | async-start | bytes 2097152 | tf_op jit(solution)/shard_map/all_to_all | solution.py:108
  257.6 79.4 %all-gather.13.cloned.1.call-start = ((), (), s32[]{:S(2)}) async-start(), calls=%async_computation.13 | async-start | bytes 3145728 | tf_op jit(solution)/shard_map/all_gather | solution.py:51
  262.2 4.3 copy-start.4
  293.7 29.1 %all-to-all-start.8 = ((bf16[16,2,16384]{2,1,0:T(2,128)(2,1)}), bf16[16,2,16384]{2,1,0:T(2,128)(2,1)S(1)}, u32[]{:S(2)}, u32[]{:S(2)}) async-start(bf16[16,2,16384]{2,1,0:T(2,128)(2,1)} %reshape.349), calls=%async_computation.8 | async-start | bytes 2097152 | tf_op jit(solution)/shard_map/all_to_all | solution.py:109
  299.7 52.0 %all-gather.15.cloned.1.call-start = ((), (), s32[]{:S(2)}) async-start(), calls=%async_computation.14 | async-start | bytes 3145728 | tf_op jit(solution)/shard_map/all_gather | solution.py:56
  322.8 72.7 %all-to-all-start.1 = ((bf16[16,30,2048]{2,1,0:T(8,128)(2,1)}), bf16[16,30,2048]{2,1,0:T(8,128)(2,1)}, u32[]{:S(2)}, u32[]{:S(2)}) async-start(bf16[16,30,2048]{2,1,0:T(8,128)(2,1)} %reshape.254), calls=%async_computation.1 | async-start | bytes 4194304 | tf_op jit(solution)/shard_map/all_to_all | solution.py:124
  329.6 57.2 %all-gather.17.cloned.1.call-start = ((), (), s32[]{:S(2)}) async-start(), calls=%async_computation.15 | async-start | bytes 3145728 | tf_op jit(solution)/shard_map/all_gather | solution.py:63
  395.5 7.2 %copy-start.11 = (f32[2,40,8]{1,2,0:T(8,128)S(1)}, f32[2,40,8]{1,2,0:T(8,128)}, u32[]{:S(2)}) copy-start(f32[2,40,8]{1,2,0:T(8,128)} %param.16) | copy-start | bytes 7684
  395.5 7.6 %copy-start.13 = (s32[2,1,4]{2,1,0:T(1,128)S(1)}, s32[2,1,4]{2,1,0:T(1,128)}, u32[]{:S(2)}) copy-start(s32[2,1,4]{2,1,0:T(1,128)} %param.24) | copy-start | bytes 100
  395.5 47.0 %all-to-all-start.9 = ((bf16[16,30,2048]{2,1,0:T(8,128)(2,1)}), bf16[16,30,2048]{2,1,0:T(8,128)(2,1)}, u32[]{:S(2)}, u32[]{:S(2)}) async-start(bf16[16,30,2048]{2,1,0:T(8,128)(2,1)} %reshape.265), calls=%async_computation.9 | async-start | bytes 4194304 | tf_op jit(solution)/shard_map/all_to_all | solution.py:124
  446.7 1.3 copy-start.6
  446.7 74.6 %copy-start.9 = (f32[2048]{0:T(1024)S(1)}, f32[2048]{0:T(1024)}, u32[]{:S(2)}) copy-start(f32[2048]{0:T(1024)} %param.18) | copy-start | bytes 24580
  449.1 76.1 %copy-start.8 = (bf16[2,40,2048]{2,1,0:T(8,128)(2,1)}, bf16[2,40,2048]{2,1,0:T(8,128)(2,1)S(1)}, u32[]{:S(2)}) copy-start(bf16[2,40,2048]{2,1,0:T(8,128)(2,1)S(1)} %pad_maximum_fusion) | copy-start | bytes 983044
Sparse Core Ops, SparseCore 0:
  177.6 34.3 all-gather.6
  213.6 33.1 all-gather.10
  248.3 33.1 all-gather.8
  283.4 33.1 all-gather.12
  318.5 33.1 all-gather.14
  353.6 33.1 all-gather.16
where the time goes:
time: 619 us; the launch traced here: 612 us
  waiting for transfers between devices  178 us (29%)
  blocking collectives  150 us (24%)
  local copies, waits for them, and re-layouts  103 us (17%)
  starting transfers between devices  77.6 us (13%)
  other arithmetic  61.8 us (10%)
  matrix products  26.1 us (4%)
  between operations  15.2 us (2%)
    psum x1, blocking collectives, per_device(): group_tails = lax.psum(tail_terms.astype(jnp.bfloat16), 'ep')  67.3 us
    unnamed x6, other arithmetic  51.2 us
    unnamed x51, local copies, waits for them, and re-layouts  47.4 us
    all_to_all x2, waiting for transfers between devices, per_device(): lax.all_to_all(sends, 'ep', split_axis=0, concat_axis=0, tiled=True)  46.2 us
    psum x1, blocking collectives, per_device(): lax.psum(jnp.sum(jnp.exp(logits - top_val[:, None]), axis=1), ('grp', 'ep'))  41.4 us
    pmax x1, blocking collectives, per_device(): top_val = lax.pmax(jnp.max(logits, axis=1), ('grp', 'ep'))  36.9 us
    all_gather x2, waiting for transfers between devices, expert_block(): lax.all_gather(down_part, 'grp', axis=1, tiled=True)[0]  35.1 us
    all_to_all x2, waiting for transfers between devices, per_device(): lax.all_to_all(results.reshape(n_dest, capacity, width), 'ep', split_axis...  32.9 us
  transfers between devices with their start and end apart: 16, of which 9 were waited for; matrix products, arithmetic and copies ran while one was open for 26% of the time, Pallas kernels for 0%

commit v1 on v0

v1 whole, which is shorter than its diff:
```python
import jax
import jax.numpy as jnp
from jax import lax
from jax.sharding import PartitionSpec as P


def normalize(rows, gain):
    scale = lax.rsqrt(jnp.mean(rows * rows, axis=-1, keepdims=True) + 1e-06)
    return (rows * scale * gain).astype(jnp.bfloat16)


def owner_table(placement):
    ident = jnp.arange(placement.shape[0], dtype=jnp.int32)
    hits = placement[None, :] == ident[:, None]
    return jnp.sum(jnp.where(hits, ident[None, :], 0), axis=1)


def exchange(value, axis, bit):
    n = lax.axis_size(axis)
    return lax.ppermute(value, axis, [(i, i ^ bit) for i in range(n)])


def relocate(weights, source):
    n = source.shape[0]
    rows = weights.reshape(n, weights.shape[1] // n, weights.shape[2])
    spread = lax.all_to_all(rows, "ep", split_axis=0, concat_axis=0, tiled=True)
    ordered = jnp.take(spread, source, axis=0)
    moved = lax.all_to_all(ordered, "ep", split_axis=0, concat_axis=0, tiled=True)
    return moved.reshape(weights.shape)


def split_bf16(value):
    high = lax.reduce_precision(value, 8, 7)
    middle = lax.reduce_precision(value - high, 8, 7)
    low = value - high - middle
    return [part.astype(jnp.bfloat16) for part in (high, middle, low)]


def scatter_sum(terms):
    n = lax.axis_size("ep")
    me = lax.axis_index("ep")
    bit = 1
    held = terms
    while bit < n:
        pairs = held.reshape(held.shape[0] // 2, 2, *held.shape[1:])
        mine = (me // bit) % 2
        sent = lax.dynamic_index_in_dim(pairs, 1 - mine, 1, keepdims=False)
        kept = lax.dynamic_index_in_dim(pairs, mine, 1, keepdims=False)
        held = kept + exchange(sent.astype(jnp.bfloat16), "ep", bit).astype(jnp.float32)
        bit *= 2
    return held[0]


def butterfly(value, axis, join):
    bit = 1
    while bit < lax.axis_size(axis):
        value = join(value, exchange(value, axis, bit))
        bit *= 2
    return value


def join_stats(ours, theirs):
    top = jnp.maximum(ours[0], theirs[0])
    total = ours[1] * jnp.exp(ours[0] - top) + theirs[1] * jnp.exp(theirs[0] - top)
    return jnp.stack([top, total])


def per_device(
    states,
    route_ids,
    route_gates,
    moe_gain,
    final_gain,
    gate_proj,
    up_proj,
    down_proj,
    old_slots,
    new_slots,
    req_lengths,
    head_proj,
):
    n_ep = lax.axis_size("ep")
    n_grp = lax.axis_size("grp")
    column = lax.axis_index("ep")
    group = lax.axis_index("grp")
    batches, tok_rows, width = states.shape
    n_slots = old_slots.shape[0]
    old_owner = owner_table(old_slots)
    source = jnp.take(old_owner, new_slots)

    residual = states.astype(jnp.float32)
    normed = normalize(residual, moe_gain).reshape(-1, width)
    chosen = route_ids[..., None] == old_slots
    slot_gates = jnp.sum(jnp.where(chosen, route_gates[..., None], 0.0), axis=2)
    parts = split_bf16(slot_gates.reshape(-1, n_slots))
    extra = -(-len(parts) * n_slots // 128) * 128
    coded = jnp.pad(jnp.concatenate(parts, axis=1), ((0, 0), (0, extra - len(parts) * n_slots)))
    rows = lax.all_gather(
        jnp.concatenate([normed, coded], axis=1), "ep", axis=0, tiled=True
    )
    gate_full = lax.all_gather(gate_proj[0], "grp", axis=0, tiled=True)
    up_full = lax.all_gather(up_proj[0], "grp", axis=0, tiled=True)
    down_full = lax.all_gather(down_proj[0], "grp", axis=0, tiled=True)

    tokens = rows[:, :width]
    codes = rows[:, width : width + len(parts) * n_slots].astype(jnp.float32)
    codes = codes.reshape(-1, len(parts), n_slots)
    own = jnp.arange(n_slots, dtype=jnp.int32) == column
    weight = jnp.sum(jnp.where(own, codes, 0.0), axis=(1, 2))
    gate_vals = jnp.dot(tokens, gate_full, preferred_element_type=jnp.float32)
    up_vals = jnp.dot(tokens, up_full, preferred_element_type=jnp.float32)
    hidden = (jax.nn.silu(gate_vals) * up_vals).astype(jnp.bfloat16)
    outputs = jnp.dot(hidden, down_full, preferred_element_type=jnp.float32)
    terms = (outputs * weight[:, None]).reshape(n_ep, -1, width)
    summed = scatter_sum(terms).reshape(states.shape)
    mixed = (residual + summed).astype(jnp.bfloat16)

    moved = tuple(relocate(weights, source) for weights in (gate_proj, up_proj, down_proj))

    request_ends = jnp.cumsum(req_lengths[:, 0, :], axis=-1) - 1
    local_ends = request_ends - column * tok_rows
    picker = (
        local_ends[:, :, None] == jnp.arange(tok_rows, dtype=jnp.int32)[None, None, :]
    ).astype(jnp.bfloat16)
    tails = jnp.einsum(
        "brt,btd->brd", picker, mixed, preferred_element_type=jnp.float32
    ).astype(jnp.bfloat16)
    add = lambda a, b: a + b
    tails = butterfly(tails, "ep", add)
    here = (jnp.arange(n_grp, dtype=jnp.int32) == group)[None, :, None, None]
    spread = jnp.where(here, tails[:, None], jnp.zeros((), jnp.bfloat16))
    spread = butterfly(spread, "grp", add)
    finals = normalize(spread.reshape(-1, width).astype(jnp.float32), final_gain)
    logits = jnp.dot(finals, head_proj, preferred_element_type=jnp.float32)
    top = jnp.max(logits, axis=1)
    total = jnp.sum(jnp.exp(logits - top[:, None]), axis=1)
    stats = jnp.stack([top, total])
    stats = butterfly(stats, "ep", join_stats)
    stats = butterfly(stats, "grp", join_stats)
    log_probs = (logits - stats[0][:, None] - jnp.log(stats[1])[:, None]).reshape(
        batches, -1, logits.shape[1]
    )
    return (mixed, *moved, log_probs)


def solution(mesh):
    placed = (
        P(None, ("grp", "ep"), None),
        P(None, ("grp", "ep"), None),
        P(None, ("grp", "ep"), None),
        P(),
        P(),
        P("ep", "grp", None),
        P("ep", "grp", None),
        P("ep", "grp", None),
        P(),
        P(),
        P(None, "grp", None),
        P(None, ("grp", "ep")),
    )
    return jax.shard_map(
        per_device,
        mesh=mesh,
        in_specs=placed,
        out_specs=(
            P(None, ("grp", "ep"), None),
            P("ep", "grp", None),
            P("ep", "grp", None),
            P("ep", "grp", None),
            P(None, None, ("grp", "ep")),
        ),
        check_vma=False,
    )
```

time: 619 us -> 422 us (0.68)
  blocking collectives: 150 us -> 30.5 us
  waiting for transfers between devices: 178 us -> 264 us
  local copies, waits for them, and re-layouts: 103 us -> 21.7 us
  other arithmetic: 61.8 us -> 20.1 us
  starting transfers between devices: 77.6 us -> 49.4 us
    all_to_all x10 -> x5, waiting for transfers between devices: 129 us -> 14.4 us  [the longest x2 14.4 us: relocate(): spread = lax.all_to_all(rows, 'ep', split_axis=0, concat_axis=0, tiled=True)]
    psum x2 -> x0, blocking collectives: 109 us -> none  [the longest x1 67.3 us: per_device(): group_tails = lax.psum(tail_terms.astype(jnp.bfloat16), 'ep')]
    all_gather x6 -> x4, waiting for transfers between devices: 47 us -> 154 us  [the longest x1 58.4 us: per_device(): lax.all_gather(jnp.concatenate([normed, coded], axis=1), 'ep', axis=0, ti...]
    ppermute x0 -> x14, waiting for transfers between devices: none -> 93.3 us  [exchange(): return lax.ppermute(value, axis, [(i, i ^ bit) for i in range(n)])]
    all_to_all x10 -> x5, starting transfers between devices: 76.7 us -> 24.5 us  [the longest x3 12.6 us: relocate(): lax.all_to_all(ordered, 'ep', split_axis=0, concat_axis=0, tiled=True)]
    unnamed x6 -> x0, other arithmetic: 51.2 us -> none
    unnamed x51 -> x24, local copies, waits for them, and re-layouts: 47.4 us -> 7.71 us
    pmax x1 -> x0, blocking collectives: 36.9 us -> none  [per_device(): top_val = lax.pmax(jnp.max(logits, axis=1), ('grp', 'ep'))]
  transfers between devices with their start and end apart: 16 -> 23, of which waited for: 9 -> 18; matrix products, arithmetic and copies ran while one was open for 26% -> 8% of each run, Pallas kernels for 0% -> 0%
where the time goes in v1:
time: 422 us; the launch traced here: 421 us
  waiting for transfers between devices  264 us (63%)
  starting transfers between devices  49.4 us (12%)
  blocking collectives  30.5 us (7%)
  local copies, waits for them, and re-layouts  21.7 us (5%)
  matrix products  20.9 us (5%)
  other arithmetic  20.1 us (5%)
  between operations  14.3 us (3%)
    ppermute x14, waiting for transfers between devices, exchange(): return lax.ppermute(value, axis, [(i, i ^ bit) for i in range(n)])  93.3 us
    all_gather x1, waiting for transfers between devices, per_device(): lax.all_gather(jnp.concatenate([normed, coded], axis=1), 'ep', axis=0, ti...  58.4 us
    all_gather x1, waiting for transfers between devices, per_device(): up_full = lax.all_gather(up_proj[0], 'grp', axis=0, tiled=True)  34.6 us
    all_gather x1, waiting for transfers between devices, per_device(): gate_full = lax.all_gather(gate_proj[0], 'grp', axis=0, tiled=True)  32.1 us
    all_to_all x1, blocking collectives, relocate(): spread = lax.all_to_all(rows, 'ep', split_axis=0, concat_axis=0, tiled=True)  30.5 us
    all_gather x1, waiting for transfers between devices, per_device(): down_full = lax.all_gather(down_proj[0], 'grp', axis=0, tiled=True)  29.3 us
    ppermute x14, starting transfers between devices, exchange(): return lax.ppermute(value, axis, [(i, i ^ bit) for i in range(n)])  24.7 us
    all_to_all x2, waiting for transfers between devices, relocate(): spread = lax.all_to_all(rows, 'ep', split_axis=0, concat_axis=0, tiled=True)  14.4 us
  transfers between devices with their start and end apart: 23, of which 18 were waited for; matrix products, arithmetic and copies ran while one was open for 8% of the time, Pallas kernels for 0%

profile of v1, /device:TPU:0, one launch (start us, length us, event | category | flops | bytes accessed | tf_op | source)
XLA Modules:
  0.0 420.9 jit_solution(121535099977191811)
XLA Ops:
  13.5 58.4 %all-gather.8.cloned.1.call-done = bf16[1280,2176]{1,0:T(8,128)(2,1)} async-done(((bf16[80,2176]{1,0:T(8,128)(2,1)}), bf16[1280,2176]{1,0:T(8,128)(2,1)}) %all-gather.8.cloned.1.call-update) | async-done | bytes 5570576 | tf_op jit(solution)/shard_map/all_gather | solution.py:98
  73.1 32.1 %all-gather.10.cloned.1.call-done = bf16[1,2048,512]{2,1,0:T(8,128)(2,1)} async-done(((bf16[1,1024,512]{2,1,0:T(8,128)(2,1)}), bf16[1,2048,512]{2,1,0:T(8,128)(2,1)}) %all-gather.10.cloned.1.call-update) | async-done | bytes 2097168 | tf_op jit(solution)/shard_map/all_gather | solution.py:101
  105.2 5.4 %fusion.2 = f32[1280,512]{1,0:T(8,128)S(1)} fusion(bf16[1280,2176]{1,0:T(8,128)(2,1)} %all-gather.8.cloned.1.call-done, bf16[1,2048,512]{2,1,0:T(8,128)(2,1)} %all-gather.10.cloned.1.call-done), kind=kOutput, calls=%fused_computation.9 | convolution fusion | flops 2684354560 | bytes 9961472 | tf_op jit(solution)/shard_map/dot_general | solution.py:110
  110.6 29.3 %all-gather.14.cloned.1.call-done = bf16[1,512,2048]{2,1,0:T(8,128)(2,1)} async-done(((bf16[1,256,2048]{2,1,0:T(8,128)(2,1)}), bf16[1,512,2048]{2,1,0:T(8,128)(2,1)}) %all-gather.14.cloned.1.call-update) | async-done | bytes 2097168 | tf_op jit(solution)/shard_map/all_gather | solution.py:103
  139.9 34.6 %all-gather.12.cloned.1.call-done = bf16[1,2048,512]{2,1,0:T(8,128)(2,1)} async-done(((bf16[1,1024,512]{2,1,0:T(8,128)(2,1)}), bf16[1,2048,512]{2,1,0:T(8,128)(2,1)}) %all-gather.12.cloned.1.call-update) | async-done | bytes 2097168 | tf_op jit(solution)/shard_map/all_gather | solution.py:102
  174.5 11.4 %convolution_multiply_fusion = f32[1280,2048]{1,0:T(8,128)} fusion(f32[1280]{0:T(1024)S(1)} %select_reduce_fusion, bf16[1,512,2048]{2,1,0:T(8,128)(2,1)} %all-gather.14.cloned.1.call-done, bf16[1280,2176]{1,0:T(8,128)(2,1)} %all-gather.8.cloned.1.call-done, f32[1280,512]{1,0:T(8,128)S(1)} %fusion.2, bf16[1,2048,512]{2,1,0:T(8,128)(2,1)} %all-gather.12.cloned.1.call-done), kind=kOutput, calls=%fused_computation.4 | convolution fusion | flops 5375262720 | bytes 22549504 | tf_op jit(solution)/shard_map/dot_general | solution.py:113
  185.9 4.5 %fusion.10 = bf16[8,80,2048]{2,1,0:T(8,128)(2,1)} fusion(f32[8,2,80,2048]{3,2,1,0:T(8,128)} %bitcast.149, s32[]{:T(128)S(6)} %select_n.112), kind=kLoop, calls=%fused_computation.13 | loop fusion | bytes 5242884 | tf_op jit(solution)/shard_map/convert_element_type | solution.py:49
  190.3 30.5 %all_to_all.30 = bf16[16,64,512]{2,1,0:T(8,128)(2,1)} all-to-all(bf16[16,64,512]{2,1,0:T(8,128)(2,1)S(1)} %bitcast.151), channel_id=1, replica_groups=mesh['grp'=2,'ep'=16] {'ep'}, dimensions={0} | all-to-all | bytes 2097152 | tf_op jit(solution)/shard_map/all_to_all | solution.py:26
  220.8 5.0 %all-to-all-start = ((bf16[16,64,512]{2,1,0:T(8,128)(2,1)}), bf16[16,64,512]{2,1,0:T(8,128)(2,1)S(1)}, u32[]{:S(2)}, u32[]{:S(2)}) async-start(bf16[16,64,512]{2,1,0:T(8,128)(2,1)} %bitcast.14), calls=%async_computation | async-start | bytes 2097152 | tf_op jit(solution)/shard_map/all_to_all | solution.py:26
  225.9 4.1 bitcast_add_fusion
  234.5 14.4 %all-to-all-done = bf16[16,64,512]{2,1,0:T(8,128)(2,1)S(1)} async-done(((bf16[16,64,512]{2,1,0:T(8,128)(2,1)}), bf16[16,64,512]{2,1,0:T(8,128)(2,1)S(1)}, u32[]{:S(2)}, u32[]{:S(2)}) %all-to-all-start) | async-done | bytes 1048608 | tf_op jit(solution)/shard_map/all_to_all | solution.py:26
  248.8 7.0 %all-to-all-start.4 = ((bf16[16,16,2048]{2,1,0:T(8,128)(2,1)}), bf16[16,16,2048]{2,1,0:T(8,128)(2,1)}, u32[]{:S(2)}, u32[]{:S(2)}) async-start(bf16[16,16,2048]{2,1,0:T(8,128)(2,1)} %bitcast.18), calls=%async_computation.4 | async-start | bytes 2097152 | tf_op jit(solution)/shard_map/all_to_all | solution.py:26
  256.7 19.4 %collective-permute-done.1 = bf16[4,80,2048]{2,1,0:T(8,128)(2,1)} collective-permute-done((bf16[4,80,2048]{2,1,0:T(8,128)(2,1)S(1)}, bf16[4,80,2048]{2,1,0:T(8,128)(2,1)}, u32[]{:S(2)}, u32[]{:S(2)}) %collective-permute-start.1) | collective-permute-done | bytes 1310752 | tf_op jit(solution)/shard_map/ppermute | solution.py:20
  276.1 2.4 bitcast_add_fusion.1
  279.5 3.7 collective-permute-start.2
  283.1 2.8 gather_fusion.3
  286.0 2.8 gather_fusion.2
  288.8 3.1 broadcast_select_fusion
  291.9 5.1 %all-to-all-start.1 = ((bf16[16,64,512]{2,1,0:T(8,128)(2,1)}), bf16[16,64,512]{2,1,0:T(8,128)(2,1)}, u32[]{:S(2)}, u32[]{:S(2)}) async-start(bf16[16,64,512]{2,1,0:T(8,128)(2,1)} %get-tuple-element.22), calls=%async_computation.1 | async-start | bytes 2097152 | tf_op jit(solution)/shard_map/all_to_all | solution.py:28
  302.4 35.1 %collective-permute-done.3 = bf16[1,80,2048]{2,1,0:T(8,128)(2,1)S(1)} collective-permute-done((bf16[1,80,2048]{2,1,0:T(8,128)(2,1)S(1)}, bf16[1,80,2048]{2,1,0:T(8,128)(2,1)S(1)}, u32[]{:S(2)}, u32[]{:S(2)}) %collective-permute-start.3) | collective-permute-done | bytes 327712 | tf_op jit(solution)/shard_map/ppermute | solution.py:20
  338.7 3.7 all-to-all-start.3
  346.0 5.7 %collective-permute-done.5 = bf16[2,4,2048]{2,1,0:T(4,128)(2,1)S(1)} collective-permute-done((bf16[2,4,2048]{2,1,0:T(4,128)(2,1)S(1)}, bf16[2,4,2048]{2,1,0:T(4,128)(2,1)S(1)}, u32[]{:S(2)}, u32[]{:S(2)}) %collective-permute-start.5) | collective-permute-done | bytes 32800 | tf_op jit(solution)/shard_map/ppermute | solution.py:20
  351.8 9.5 %collective-permute-done.6 = bf16[2,4,2048]{2,1,0:T(4,128)(2,1)S(1)} collective-permute-done((bf16[2,4,2048]{2,1,0:T(4,128)(2,1)S(1)}, bf16[2,4,2048]{2,1,0:T(4,128)(2,1)S(1)}, u32[]{:S(2)}, u32[]{:S(2)}) %collective-permute-start.6) | collective-permute-done | bytes 32800 | tf_op jit(solution)/shard_map/ppermute | solution.py:20
  361.3 4.5 %collective-permute-start.7 = (bf16[2,4,2048]{2,1,0:T(4,128)(2,1)S(1)}, bf16[2,4,2048]{2,1,0:T(4,128)(2,1)S(1)}, u32[]{:S(2)}, u32[]{:S(2)}) collective-permute-start(bf16[2,4,2048]{2,1,0:T(4,128)(2,1)S(1)} %add.202), channel_id=1, source_target_pairs={{0,8},{1,9},{2,10},{3,11},{4,12},{5,13},{6,14},{7,15},{8,0},{9,1},... | collective-permute-start | bytes 98312 | tf_op jit(solution)/shard_map/ppermute | solution.py:20
  367.6 2.8 collective-permute-done.7
  372.3 2.6 collective-permute-done.8
  375.4 3.7 all-to-all-start.5
  379.1 3.9 fusion.47
  390.1 7.2 %collective-permute-done.11 = f32[2,16]{1,0:T(2,128)S(1)} collective-permute-done((f32[2,16]{1,0:T(2,128)S(1)}, f32[2,16]{1,0:T(2,128)S(1)}, u32[]{:S(2)}, u32[]{:S(2)}) %collective-permute-start.11) | collective-permute-done | bytes 160 | tf_op jit(solution)/shard_map/ppermute | solution.py:20
  397.3 4.4 %collective-permute-start.12 = (f32[2,16]{1,0:T(2,128)S(1)}, f32[2,16]{1,0:T(2,128)S(1)}, u32[]{:S(2)}, u32[]{:S(2)}) collective-permute-start(f32[2,16]{1,0:T(2,128)S(1)} %pad_maximum_fusion.4), channel_id=1, source_target_pairs={{0,8},{1,9},{2,10},{3,11},{4,12},{5,13},{6,14},{7,15},{8,0},{9,1},... | collective-permute-start | bytes 392 | tf_op jit(solution)/shard_map/ppermute | solution.py:20
  401.7 4.0 collective-permute-done.12
  406.4 3.0 collective-permute-done.13
  (105 shorter events, 40.7 us)
Async XLA Ops:
  7.2 64.8 %all-gather.8.cloned.1.call-start = ((), (), s32[]{:S(2)}) async-start(), calls=%async_computation.6 | async-start | bytes 5918720 | tf_op jit(solution)/shard_map/all_gather | solution.py:98
  11.3 93.9 %all-gather.10.cloned.1.call-start = ((), (), s32[]{:S(2)}) async-start(), calls=%async_computation.7 | async-start | bytes 3145728 | tf_op jit(solution)/shard_map/all_gather | solution.py:101
  12.1 127.8 %all-gather.14.cloned.1.call-start = ((), (), s32[]{:S(2)}) async-start(), calls=%async_computation.9 | async-start | bytes 3145728 | tf_op jit(solution)/shard_map/all_gather | solution.py:103
  12.8 161.7 %all-gather.12.cloned.1.call-start = ((), (), s32[]{:S(2)}) async-start(), calls=%async_computation.8 | async-start | bytes 3145728 | tf_op jit(solution)/shard_map/all_gather | solution.py:102
  185.9 4.5 %copy-start.2 = (bf16[1,1024,512]{2,1,0:T(8,128)(2,1)S(1)}, bf16[1,1024,512]{2,1,0:T(8,128)(2,1)}, u32[]{:S(2)}) copy-start(bf16[1,1024,512]{2,1,0:T(8,128)(2,1)} %param.20) | copy-start | bytes 3145732
  190.3 35.5 %collective-permute-start = (bf16[8,80,2048]{2,1,0:T(8,128)(2,1)}, bf16[8,80,2048]{2,1,0:T(8,128)(2,1)}, u32[]{:S(2)}, u32[]{:S(2)}) collective-permute-start(bf16[8,80,2048]{2,1,0:T(8,128)(2,1)} %fusion.10), channel_id=1, source_target_pairs={{0,1},{1,0},{2,3},{3,2},{4,5},{5,4},{6,7},{7,6},{8,9},{9,8},{10,11... | collective-permute-start | bytes 7864328 | tf_op jit(solution)/shard_map/ppermute | solution.py:20
  220.8 28.0 %all-to-all-start = ((bf16[16,64,512]{2,1,0:T(8,128)(2,1)}), bf16[16,64,512]{2,1,0:T(8,128)(2,1)S(1)}, u32[]{:S(2)}, u32[]{:S(2)}) async-start(bf16[16,64,512]{2,1,0:T(8,128)(2,1)} %bitcast.14), calls=%async_computation | async-start | bytes 2097152 | tf_op jit(solution)/shard_map/all_to_all | solution.py:26
  230.0 2.3 copy-start
  230.0 25.9 %copy-start.9 = (s32[16]{0:T(128)S(1)}, s32[16]{0:T(128)}, u32[]{:S(2)}) copy-start(s32[16]{0:T(128)} %param.23) | copy-start | bytes 196
  230.0 25.9 %copy-start.8 = (s32[16]{0:T(128)S(1)}, s32[16]{0:T(128)}, u32[]{:S(2)}) copy-start(s32[16]{0:T(128)} %param.22) | copy-start | bytes 196
  232.5 43.6 %collective-permute-start.1 = (bf16[4,80,2048]{2,1,0:T(8,128)(2,1)S(1)}, bf16[4,80,2048]{2,1,0:T(8,128)(2,1)}, u32[]{:S(2)}, u32[]{:S(2)}) collective-permute-start(bf16[4,80,2048]{2,1,0:T(8,128)(2,1)S(1)} %fusion.14), channel_id=1, source_target_pairs={{0,2},{1,3},{2,0},{3,1},{4,6},{5,7},{6,4},{7,5},{8,10},{9,11},{10,... | collective-permute-start | bytes 3932168 | tf_op jit(solution)/shard_map/ppermute | solution.py:20
  248.8 7.1 %copy-start.1 = (bf16[16,64,512]{2,1,0:T(8,128)(2,1)}, bf16[16,64,512]{2,1,0:T(8,128)(2,1)S(1)}, u32[]{:S(2)}) copy-start(bf16[16,64,512]{2,1,0:T(8,128)(2,1)S(1)} %all-to-all-done) | copy-start | bytes 3145732
  248.8 43.1 %all-to-all-start.4 = ((bf16[16,16,2048]{2,1,0:T(8,128)(2,1)}), bf16[16,16,2048]{2,1,0:T(8,128)(2,1)}, u32[]{:S(2)}, u32[]{:S(2)}) async-start(bf16[16,16,2048]{2,1,0:T(8,128)(2,1)} %bitcast.18), calls=%async_computation.4 | async-start | bytes 2097152 | tf_op jit(solution)/shard_map/all_to_all | solution.py:26
  279.5 18.2 %collective-permute-start.2 = (bf16[2,80,2048]{2,1,0:T(8,128)(2,1)}, bf16[2,80,2048]{2,1,0:T(8,128)(2,1)}, u32[]{:S(2)}, u32[]{:S(2)}) collective-permute-start(bf16[2,80,2048]{2,1,0:T(8,128)(2,1)} %fusion.24), channel_id=1, source_target_pairs={{0,4},{1,5},{2,6},{3,7},{4,0},{5,1},{6,2},{7,3},{8,12},{9,13},{10,... | collective-permute-start | bytes 1966088 | tf_op jit(solution)/shard_map/ppermute | solution.py:20
  291.9 10.3 %copy-start.7 = (s32[2,1,4]{2,1,0:T(1,128)S(1)}, s32[2,1,4]{2,1,0:T(1,128)}, u32[]{:S(2)}) copy-start(s32[2,1,4]{2,1,0:T(1,128)} %param.24) | copy-start | bytes 100
  291.9 46.9 %all-to-all-start.1 = ((bf16[16,64,512]{2,1,0:T(8,128)(2,1)}), bf16[16,64,512]{2,1,0:T(8,128)(2,1)}, u32[]{:S(2)}, u32[]{:S(2)}) async-start(bf16[16,64,512]{2,1,0:T(8,128)(2,1)} %get-tuple-element.22), calls=%async_computation.1 | async-start | bytes 2097152 | tf_op jit(solution)/shard_map/all_to_all | solution.py:28
  297.0 41.7 %copy-start.4 = (bf16[2,40,2048]{2,1,0:T(8,128)(2,1)S(1)}, bf16[2,40,2048]{2,1,0:T(8,128)(2,1)}, u32[]{:S(2)}) copy-start(bf16[2,40,2048]{2,1,0:T(8,128)(2,1)} %param.14) | copy-start | bytes 983044
  300.0 37.5 %collective-permute-start.3 = (bf16[1,80,2048]{2,1,0:T(8,128)(2,1)S(1)}, bf16[1,80,2048]{2,1,0:T(8,128)(2,1)S(1)}, u32[]{:S(2)}, u32[]{:S(2)}) collective-permute-start(bf16[1,80,2048]{2,1,0:T(8,128)(2,1)S(1)} %dynamic-slice_convert_fusion.2), channel_id=1, source_target_pairs={{0,8},{1,9},{2,10},{3,11},{4,12},{5,13},{6,14},{7,15},{8,0},{9,1},... | collective-permute-start | bytes 983048 | tf_op jit(solution)/shard_map/ppermute | solution.py:20
  338.7 33.6 %copy-start.5 = (bf16[2,40,2048]{2,1,0:T(8,128)(2,1)}, bf16[2,40,2048]{2,1,0:T(8,128)(2,1)S(1)}, u32[]{:S(2)}) copy-start(bf16[2,40,2048]{2,1,0:T(8,128)(2,1)S(1)} %fusion.23) | copy-start | bytes 983044
  338.7 36.6 %all-to-all-start.3 = ((bf16[16,64,512]{2,1,0:T(8,128)(2,1)}), bf16[16,64,512]{2,1,0:T(8,128)(2,1)S(1)}, u32[]{:S(2)}, u32[]{:S(2)}) async-start(bf16[16,64,512]{2,1,0:T(8,128)(2,1)} %get-tuple-element.21), calls=%async_computation.3 | async-start | bytes 2097152 | tf_op jit(solution)/shard_map/all_to_all | solution.py:28
  342.7 1.3 collective-permute-start.4
  344.1 7.6 %collective-permute-start.5 = (bf16[2,4,2048]{2,1,0:T(4,128)(2,1)S(1)}, bf16[2,4,2048]{2,1,0:T(4,128)(2,1)S(1)}, u32[]{:S(2)}, u32[]{:S(2)}) collective-permute-start(bf16[2,4,2048]{2,1,0:T(4,128)(2,1)S(1)} %add.200), channel_id=1, source_target_pairs={{0,2},{1,3},{2,0},{3,1},{4,6},{5,7},{6,4},{7,5},{8,10},{9,11},{10,... | collective-permute-start | bytes 98312 | tf_op jit(solution)/shard_map/ppermute | solution.py:20
  351.8 9.5 %collective-permute-start.6 = (bf16[2,4,2048]{2,1,0:T(4,128)(2,1)S(1)}, bf16[2,4,2048]{2,1,0:T(4,128)(2,1)S(1)}, u32[]{:S(2)}, u32[]{:S(2)}) collective-permute-start(bf16[2,4,2048]{2,1,0:T(4,128)(2,1)S(1)} %add.201), channel_id=1, source_target_pairs={{0,4},{1,5},{2,6},{3,7},{4,0},{5,1},{6,2},{7,3},{8,12},{9,13},{10,... | collective-permute-start | bytes 98312 | tf_op jit(solution)/shard_map/ppermute | solution.py:20
  361.3 9.1 %collective-permute-start.7 = (bf16[2,4,2048]{2,1,0:T(4,128)(2,1)S(1)}, bf16[2,4,2048]{2,1,0:T(4,128)(2,1)S(1)}, u32[]{:S(2)}, u32[]{:S(2)}) collective-permute-start(bf16[2,4,2048]{2,1,0:T(4,128)(2,1)S(1)} %add.202), channel_id=1, source_target_pairs={{0,8},{1,9},{2,10},{3,11},{4,12},{5,13},{6,14},{7,15},{8,0},{9,1},... | collective-permute-start | bytes 98312 | tf_op jit(solution)/shard_map/ppermute | solution.py:20
  367.6 11.5 %copy-start.6 = (f32[2048]{0:T(1024)S(1)}, f32[2048]{0:T(1024)}, u32[]{:S(2)}) copy-start(f32[2048]{0:T(1024)} %param.18) | copy-start | bytes 24580
  370.6 4.3 %collective-permute-start.8 = (bf16[2,2,4,2048]{3,2,1,0:T(4,128)(2,1)S(1)}, bf16[2,2,4,2048]{3,2,1,0:T(4,128)(2,1)S(1)}, u32[]{:S(2)}, u32[]{:S(2)}) collective-permute-start(bf16[2,2,4,2048]{3,2,1,0:T(4,128)(2,1)S(1)} %broadcast_select_fusion.3), channel_id=1, source_target_pairs={{0,16},{16,0},{1,17},{17,1},{2,18},{18,2},{3,19},{19,3},{4,20},{20... | collective-permute-start | bytes 196616 | tf_op jit(solution)/shard_map/ppermute | solution.py:20
  375.4 31.0 %all-to-all-start.5 = ((bf16[16,16,2048]{2,1,0:T(8,128)(2,1)}), bf16[16,16,2048]{2,1,0:T(8,128)(2,1)S(1)}, u32[]{:S(2)}, u32[]{:S(2)}) async-start(bf16[16,16,2048]{2,1,0:T(8,128)(2,1)} %broadcast_select_fusion.2), calls=%async_computation.5 | async-start | bytes 2097152 | tf_op jit(solution)/shard_map/all_to_all | solution.py:28
  383.2 1.3 collective-permute-start.9
  384.5 3.6 collective-permute-start.10
  388.2 9.1 %collective-permute-start.11 = (f32[2,16]{1,0:T(2,128)S(1)}, f32[2,16]{1,0:T(2,128)S(1)}, u32[]{:S(2)}, u32[]{:S(2)}) collective-permute-start(f32[2,16]{1,0:T(2,128)S(1)} %pad_maximum_fusion.3), channel_id=1, source_target_pairs={{0,4},{1,5},{2,6},{3,7},{4,0},{5,1},{6,2},{7,3},{8,12},{9,13},{10,... | collective-permute-start | bytes 392 | tf_op jit(solution)/shard_map/ppermute | solution.py:20
  397.3 8.4 %collective-permute-start.12 = (f32[2,16]{1,0:T(2,128)S(1)}, f32[2,16]{1,0:T(2,128)S(1)}, u32[]{:S(2)}, u32[]{:S(2)}) collective-permute-start(f32[2,16]{1,0:T(2,128)S(1)} %pad_maximum_fusion.4), channel_id=1, source_target_pairs={{0,8},{1,9},{2,10},{3,11},{4,12},{5,13},{6,14},{7,15},{8,0},{9,1},... | collective-permute-start | bytes 392 | tf_op jit(solution)/shard_map/ppermute | solution.py:20
  405.7 3.6 collective-permute-start.13
  (1 other events, 1.1 us)
Sparse Core Ops, SparseCore 0:
  11.4 60.4 all-gather.7
  73.5 31.6 all-gather.9
  106.7 33.1 all-gather.13
  141.3 33.1 all-gather.11

commit v2 on v1

--- a/solution.py
+++ b/solution.py
@@ -20,13 +20,28 @@
     return lax.ppermute(value, axis, [(i, i ^ bit) for i in range(n)])
 
 
-def relocate(weights, source):
-    n = source.shape[0]
+def spread_rows(weights):
+    n = lax.axis_size("ep")
     rows = weights.reshape(n, weights.shape[1] // n, weights.shape[2])
-    spread = lax.all_to_all(rows, "ep", split_axis=0, concat_axis=0, tiled=True)
+    return lax.all_to_all(rows, "ep", split_axis=0, concat_axis=0, tiled=True)
+
+
+def relocate(spread, source, shape):
     ordered = jnp.take(spread, source, axis=0)
     moved = lax.all_to_all(ordered, "ep", split_axis=0, concat_axis=0, tiled=True)
-    return moved.reshape(weights.shape)
+    return moved.reshape(shape)
+
+
+def gather_rows(held, axis):
+    bit = 1
+    while bit < lax.axis_size(axis):
+        theirs = exchange(held, axis, bit)
+        upper = (lax.axis_index(axis) // bit) % 2 == 1
+        held = jnp.concatenate(
+            [jnp.where(upper, theirs, held), jnp.where(upper, held, theirs)], axis=0
+        )
+        bit *= 2
+    return held
 
 
 def split_bf16(value):
@@ -98,9 +113,11 @@
     rows = lax.all_gather(
         jnp.concatenate([normed, coded], axis=1), "ep", axis=0, tiled=True
     )
-    gate_full = lax.all_gather(gate_proj[0], "grp", axis=0, tiled=True)
-    up_full = lax.all_gather(up_proj[0], "grp", axis=0, tiled=True)
-    down_full = lax.all_gather(down_proj[0], "grp", axis=0, tiled=True)
+    gate_full = gather_rows(gate_proj[0], "grp")
+    up_full = gather_rows(up_proj[0], "grp")
+    down_full = gather_rows(down_proj[0], "grp")
+    spread = tuple(spread_rows(weights) for weights in (gate_proj, up_proj, down_proj))
+    rows, spread = lax.optimization_barrier((rows, spread))
 
     tokens = rows[:, :width]
     codes = rows[:, width : width + len(parts) * n_slots].astype(jnp.float32)
@@ -115,7 +132,10 @@
     summed = scatter_sum(terms).reshape(states.shape)
     mixed = (residual + summed).astype(jnp.bfloat16)
 
-    moved = tuple(relocate(weights, source) for weights in (gate_proj, up_proj, down_proj))
+    moved = tuple(
+        relocate(part, source, weights.shape)
+        for part, weights in zip(spread, (gate_proj, up_proj, down_proj))
+    )
 
     request_ends = jnp.cumsum(req_lengths[:, 0, :], axis=-1) - 1
     local_ends = request_ends - column * tok_rows
@@ -128,9 +148,9 @@
     add = lambda a, b: a + b
     tails = butterfly(tails, "ep", add)
     here = (jnp.arange(n_grp, dtype=jnp.int32) == group)[None, :, None, None]
-    spread = jnp.where(here, tails[:, None], jnp.zeros((), jnp.bfloat16))
-    spread = butterfly(spread, "grp", add)
-    finals = normalize(spread.reshape(-1, width).astype(jnp.float32), final_gain)
+    placed = jnp.where(here, tails[:, None], jnp.zeros((), jnp.bfloat16))
+    placed = butterfly(placed, "grp", add)
+    finals = normalize(placed.reshape(-1, width).astype(jnp.float32), final_gain)
     logits = jnp.dot(finals, head_proj, preferred_element_type=jnp.float32)
     top = jnp.max(logits, axis=1)
     total = jnp.sum(jnp.exp(logits - top[:, None]), axis=1)

time: 422 us -> 365 us (0.86)
  waiting for transfers between devices: 264 us -> 186 us
  blocking collectives: 30.5 us -> 43.3 us
  other arithmetic: 20.1 us -> 27.4 us
  matrix products: 20.9 us -> 15.3 us
  starting transfers between devices: 49.4 us -> 54.3 us
    all_gather x3 -> x0, waiting for transfers between devices: 95.9 us -> none  [the longest x1 34.6 us: per_device(): up_full = lax.all_gather(up_proj[0], 'grp', axis=0, tiled=True)]
    all_gather x1, waiting for transfers between devices: 58.4 us -> 0.01 us  [per_device(): lax.all_gather(jnp.concatenate([normed, coded], axis=1), 'ep', axis=0, ti...]
    ppermute x14 -> x17, waiting for transfers between devices: 93.3 us -> 148 us  [exchange(): return lax.ppermute(value, axis, [(i, i ^ bit) for i in range(n)])]
    all_to_all x2, waiting for transfers between devices: 14.4 us -> 38.3 us  [spread_rows(): return lax.all_to_all(rows, 'ep', split_axis=0, concat_axis=0, tiled=True)]
    all_to_all x1, blocking collectives: 30.5 us -> 43.3 us  [spread_rows(): return lax.all_to_all(rows, 'ep', split_axis=0, concat_axis=0, tiled=True)]
    dot_general x1, matrix products: 11.4 us -> 2.9 us  [per_device(): outputs = jnp.dot(hidden, down_full, preferred_element_type=jnp.float32)]
    select_n x1 -> x4, other arithmetic: 0.1 us -> 7.63 us  [the longest x3 7.53 us: gather_rows(): jnp.where(upper, theirs, held)]
    unnamed x24 -> x46, local copies, waits for them, and re-layouts: 7.71 us -> 12.8 us
  transfers between devices with their start and end apart: 23 -> 23, of which waited for: 18 -> 17; matrix products, arithmetic and copies ran while one was open for 8% -> 7% of each run, Pallas kernels for 0% -> 0%
where the time goes in v2:
time: 365 us; the launch traced here: 364 us
  waiting for transfers between devices  186 us (51%)
  starting transfers between devices  54.3 us (15%)
  blocking collectives  43.3 us (12%)
  other arithmetic  27.4 us (8%)
  local copies, waits for them, and re-layouts  23.1 us (6%)
  matrix products  15.3 us (4%)
  between operations  14.5 us (4%)
    ppermute x17, waiting for transfers between devices, exchange(): return lax.ppermute(value, axis, [(i, i ^ bit) for i in range(n)])  148 us
    all_to_all x1, blocking collectives, spread_rows(): return lax.all_to_all(rows, 'ep', split_axis=0, concat_axis=0, tiled=True)  43.3 us
    all_to_all x2, waiting for transfers between devices, spread_rows(): return lax.all_to_all(rows, 'ep', split_axis=0, concat_axis=0, tiled=True)  38.3 us
    ppermute x17, starting transfers between devices, exchange(): return lax.ppermute(value, axis, [(i, i ^ bit) for i in range(n)])  28.8 us
    all_to_all x2, starting transfers between devices, spread_rows(): return lax.all_to_all(rows, 'ep', split_axis=0, concat_axis=0, tiled=True)  13 us
    unnamed x46, local copies, waits for them, and re-layouts  12.8 us
    all_to_all x3, starting transfers between devices, relocate(): lax.all_to_all(ordered, 'ep', split_axis=0, concat_axis=0, tiled=True)  12.4 us
    add x4, other arithmetic, scatter_sum(): kept + exchange(sent.astype(jnp.bfloat16), 'ep', bit).astype(jnp.float32)  8.13 us
  transfers between devices with their start and end apart: 23, of which 17 were waited for; matrix products, arithmetic and copies ran while one was open for 7% of the time, Pallas kernels for 0%

profile of v2, /device:TPU:0, one launch (start us, length us, event | category | flops | bytes accessed | tf_op | source)
XLA Modules:
  0.0 363.7 jit_solution(9053971295437620537)
XLA Ops:
  11.4 43.3 %all_to_all.30 = bf16[16,64,512]{2,1,0:T(8,128)(2,1)} all-to-all(bf16[16,64,512]{2,1,0:T(8,128)(2,1)S(1)} %bitcast.150), channel_id=1, replica_groups=mesh['grp'=2,'ep'=16] {'ep'}, dimensions={0} | all-to-all | bytes 2097152 | tf_op jit(solution)/shard_map/all_to_all | solution.py:26
  54.7 4.9 %all-to-all-start.1 = ((bf16[16,64,512]{2,1,0:T(8,128)(2,1)}), bf16[16,64,512]{2,1,0:T(8,128)(2,1)S(1)}, u32[]{:S(2)}, u32[]{:S(2)}) async-start(bf16[16,64,512]{2,1,0:T(8,128)(2,1)} %bitcast.2), calls=%async_computation.1 | async-start | bytes 2097152 | tf_op jit(solution)/shard_map/all_to_all | solution.py:26
  61.2 38.3 %all-to-all-done.1 = bf16[16,64,512]{2,1,0:T(8,128)(2,1)S(1)} async-done(((bf16[16,64,512]{2,1,0:T(8,128)(2,1)}), bf16[16,64,512]{2,1,0:T(8,128)(2,1)S(1)}, u32[]{:S(2)}, u32[]{:S(2)}) %all-to-all-start.1) | async-done | bytes 1048608 | tf_op jit(solution)/shard_map/all_to_all | solution.py:26
  100.5 8.1 %all-to-all-start.2 = ((bf16[16,16,2048]{2,1,0:T(8,128)(2,1)}), bf16[16,16,2048]{2,1,0:T(8,128)(2,1)S(1)}, u32[]{:S(2)}, u32[]{:S(2)}) async-start(bf16[16,16,2048]{2,1,0:T(8,128)(2,1)} %bitcast.3), calls=%async_computation.2 | async-start | bytes 2097152 | tf_op jit(solution)/shard_map/all_to_all | solution.py:26
  112.2 22.7 %collective-permute-done.1 = bf16[1024,512]{1,0:T(8,128)(2,1)} collective-permute-done((bf16[1024,512]{1,0:T(8,128)(2,1)}, bf16[1024,512]{1,0:T(8,128)(2,1)}, u32[]{:S(2)}, u32[]{:S(2)}) %collective-permute-start.1) | collective-permute-done | bytes 1048608 | tf_op jit(solution)/shard_map/ppermute | solution.py:20
  134.9 3.0 broadcast_select_fusion.6
  138.0 18.9 %collective-permute-done.2 = bf16[256,2048]{1,0:T(8,128)(2,1)} collective-permute-done((bf16[256,2048]{1,0:T(8,128)(2,1)}, bf16[256,2048]{1,0:T(8,128)(2,1)}, u32[]{:S(2)}, u32[]{:S(2)}) %collective-permute-start.2) | collective-permute-done | bytes 1048608 | tf_op jit(solution)/shard_map/ppermute | solution.py:20
  156.8 3.1 broadcast_select_fusion.4
  161.6 5.0 %fusion.2 = f32[1280,512]{1,0:T(8,128)S(1)} fusion(bf16[1280,2176]{1,0:T(8,128)(2,1)} %all-gather.2.cloned.1.call-done, bf16[1024,512]{1,0:T(8,128)(2,1)S(1)} %copy-done.10, bf16[1024,512]{1,0:T(8,128)(2,1)S(1)} %copy-done.9), kind=kOutput, calls=%fused_computation.9 | convolution fusion | flops 2688548864 | bytes 9961472 | tf_op jit(solution)/shard_map/dot_general | solution.py:127
  166.6 3.3 multiply_convert_fusion
  169.9 2.9 convolution_multiply_fusion
  172.9 4.0 %copy-done.1 = f32[1280,2048]{1,0:T(8,128)} copy-done((f32[1280,2048]{1,0:T(8,128)}, f32[1280,2048]{1,0:T(8,128)S(1)}, u32[]{:S(2)}) %copy-start.1) | copy-done | bytes 10485784
  178.9 5.1 %collective-permute-done.3 = bf16[8,80,2048]{2,1,0:T(8,128)(2,1)S(1)} collective-permute-done((bf16[8,80,2048]{2,1,0:T(8,128)(2,1)}, bf16[8,80,2048]{2,1,0:T(8,128)(2,1)S(1)}, u32[]{:S(2)}, u32[]{:S(2)}) %collective-permute-start.3) | collective-permute-done | bytes 2621472 | tf_op jit(solution)/shard_map/ppermute | solution.py:20
  184.0 3.3 bitcast_add_fusion
  192.3 28.5 %collective-permute-done.4 = bf16[4,80,2048]{2,1,0:T(8,128)(2,1)} collective-permute-done((bf16[4,80,2048]{2,1,0:T(8,128)(2,1)S(1)}, bf16[4,80,2048]{2,1,0:T(8,128)(2,1)}, u32[]{:S(2)}, u32[]{:S(2)}) %collective-permute-start.4) | collective-permute-done | bytes 1310752 | tf_op jit(solution)/shard_map/ppermute | solution.py:20
  220.8 2.4 bitcast_add_fusion.1
  225.9 2.8 gather_fusion.2
  228.7 2.8 gather_fusion.3
  231.5 3.1 broadcast_select_fusion
  234.6 4.8 %all-to-all-start.3 = ((bf16[16,64,512]{2,1,0:T(8,128)(2,1)}), bf16[16,64,512]{2,1,0:T(8,128)(2,1)}, u32[]{:S(2)}, u32[]{:S(2)}) async-start(bf16[16,64,512]{2,1,0:T(8,128)(2,1)} %get-tuple-element.36), calls=%async_computation.3 | async-start | bytes 2097152 | tf_op jit(solution)/shard_map/all_to_all | solution.py:31
  242.8 2.6 collective-permute-start.6
  245.6 34.3 %collective-permute-done.6 = bf16[1,80,2048]{2,1,0:T(8,128)(2,1)S(1)} collective-permute-done((bf16[1,80,2048]{2,1,0:T(8,128)(2,1)S(1)}, bf16[1,80,2048]{2,1,0:T(8,128)(2,1)S(1)}, u32[]{:S(2)}, u32[]{:S(2)}) %collective-permute-start.6) | collective-permute-done | bytes 327712 | tf_op jit(solution)/shard_map/ppermute | solution.py:20
  281.2 3.9 %all-to-all-start.4 = ((bf16[16,64,512]{2,1,0:T(8,128)(2,1)}), bf16[16,64,512]{2,1,0:T(8,128)(2,1)S(1)}, u32[]{:S(2)}, u32[]{:S(2)}) async-start(bf16[16,64,512]{2,1,0:T(8,128)(2,1)} %get-tuple-element.35), calls=%async_computation.4 | async-start | bytes 2097152 | tf_op jit(solution)/shard_map/all_to_all | solution.py:31
  288.5 5.7 %collective-permute-done.8 = bf16[2,4,2048]{2,1,0:T(4,128)(2,1)S(1)} collective-permute-done((bf16[2,4,2048]{2,1,0:T(4,128)(2,1)S(1)}, bf16[2,4,2048]{2,1,0:T(4,128)(2,1)S(1)}, u32[]{:S(2)}, u32[]{:S(2)}) %collective-permute-start.8) | collective-permute-done | bytes 32800 | tf_op jit(solution)/shard_map/ppermute | solution.py:20
  294.3 9.4 %collective-permute-done.9 = bf16[2,4,2048]{2,1,0:T(4,128)(2,1)S(1)} collective-permute-done((bf16[2,4,2048]{2,1,0:T(4,128)(2,1)S(1)}, bf16[2,4,2048]{2,1,0:T(4,128)(2,1)S(1)}, u32[]{:S(2)}, u32[]{:S(2)}) %collective-permute-start.9) | collective-permute-done | bytes 32800 | tf_op jit(solution)/shard_map/ppermute | solution.py:20
  303.7 4.6 %collective-permute-start.10 = (bf16[2,4,2048]{2,1,0:T(4,128)(2,1)S(1)}, bf16[2,4,2048]{2,1,0:T(4,128)(2,1)S(1)}, u32[]{:S(2)}, u32[]{:S(2)}) collective-permute-start(bf16[2,4,2048]{2,1,0:T(4,128)(2,1)S(1)} %add.209), channel_id=1, source_target_pairs={{0,8},{1,9},{2,10},{3,11},{4,12},{5,13},{6,14},{7,15},{8,0},{9,1},... | collective-permute-start | bytes 98312 | tf_op jit(solution)/shard_map/ppermute | solution.py:20
  308.9 4.0 %collective-permute-done.10 = bf16[2,4,2048]{2,1,0:T(4,128)(2,1)S(1)} collective-permute-done((bf16[2,4,2048]{2,1,0:T(4,128)(2,1)S(1)}, bf16[2,4,2048]{2,1,0:T(4,128)(2,1)S(1)}, u32[]{:S(2)}, u32[]{:S(2)}) %collective-permute-start.10) | collective-permute-done | bytes 32800 | tf_op jit(solution)/shard_map/ppermute | solution.py:20
  317.9 3.7 %all-to-all-start.5 = ((bf16[16,16,2048]{2,1,0:T(8,128)(2,1)}), bf16[16,16,2048]{2,1,0:T(8,128)(2,1)S(1)}, u32[]{:S(2)}, u32[]{:S(2)}) async-start(bf16[16,16,2048]{2,1,0:T(8,128)(2,1)} %broadcast_select_fusion.2), calls=%async_computation.5 | async-start | bytes 2097152 | tf_op jit(solution)/shard_map/all_to_all | solution.py:31
  321.6 3.9 %fusion.49 = (f32[16]{0:T(128)S(1)}, f32[16,1536]{1,0:T(8,128)S(1)}) fusion(bf16[2048,1536]{1,0:T(8,128)(2,1)} %param.25, f32[16,2048]{1,0:T(8,128)S(1)} %reshape.265, f32[2048]{0:T(1024)S(1)} %copy-done.15, f32[16]{0:T(128)S(1)} %rsqrt.21), kind=kOutput, calls=%fused_computation.128 | convolution fusion | flops 100786160 | bytes 6529152 | tf_op jit(solution)/shard_map/dot_general | solution.py:154
  332.6 7.2 %collective-permute-done.14 = f32[2,16]{1,0:T(2,128)S(1)} collective-permute-done((f32[2,16]{1,0:T(2,128)S(1)}, f32[2,16]{1,0:T(2,128)S(1)}, u32[]{:S(2)}, u32[]{:S(2)}) %collective-permute-start.14) | collective-permute-done | bytes 160 | tf_op jit(solution)/shard_map/ppermute | solution.py:20
  339.8 4.4 %collective-permute-start.15 = (f32[2,16]{1,0:T(2,128)S(1)}, f32[2,16]{1,0:T(2,128)S(1)}, u32[]{:S(2)}, u32[]{:S(2)}) collective-permute-start(f32[2,16]{1,0:T(2,128)S(1)} %pad_maximum_fusion.4), channel_id=1, source_target_pairs={{0,8},{1,9},{2,10},{3,11},{4,12},{5,13},{6,14},{7,15},{8,0},{9,1},... | collective-permute-start | bytes 392 | tf_op jit(solution)/shard_map/ppermute | solution.py:20
  344.2 4.0 %collective-permute-done.15 = f32[2,16]{1,0:T(2,128)S(1)} collective-permute-done((f32[2,16]{1,0:T(2,128)S(1)}, f32[2,16]{1,0:T(2,128)S(1)}, u32[]{:S(2)}, u32[]{:S(2)}) %collective-permute-start.15) | collective-permute-done | bytes 160 | tf_op jit(solution)/shard_map/ppermute | solution.py:20
  (129 shorter events, 51.1 us)
Async XLA Ops:
  7.2 152.7 %all-gather.2.cloned.1.call-start = ((), (), s32[]{:S(2)}) async-start(), calls=%async_computation.6 | async-start | bytes 5918720 | tf_op jit(solution)/shard_map/all_gather | solution.py:113
  54.7 44.8 %all-to-all-start.1 = ((bf16[16,64,512]{2,1,0:T(8,128)(2,1)}), bf16[16,64,512]{2,1,0:T(8,128)(2,1)S(1)}, u32[]{:S(2)}, u32[]{:S(2)}) async-start(bf16[16,64,512]{2,1,0:T(8,128)(2,1)} %bitcast.2), calls=%async_computation.1 | async-start | bytes 2097152 | tf_op jit(solution)/shard_map/all_to_all | solution.py:26
  59.7 51.1 %collective-permute-start = (bf16[1024,512]{1,0:T(8,128)(2,1)S(1)}, bf16[1024,512]{1,0:T(8,128)(2,1)S(1)}, u32[]{:S(2)}, u32[]{:S(2)}) collective-permute-start(bf16[1024,512]{1,0:T(8,128)(2,1)S(1)} %bitcast.151), channel_id=1, source_target_pairs={{0,16},{16,0},{1,17},{17,1},{2,18},{18,2},{3,19},{19,3},{4,20},{20... | collective-permute-start | bytes 3145736 | tf_op jit(solution)/shard_map/ppermute | solution.py:20
  100.5 59.4 %all-to-all-start.2 = ((bf16[16,16,2048]{2,1,0:T(8,128)(2,1)}), bf16[16,16,2048]{2,1,0:T(8,128)(2,1)S(1)}, u32[]{:S(2)}, u32[]{:S(2)}) async-start(bf16[16,16,2048]{2,1,0:T(8,128)(2,1)} %bitcast.3), calls=%async_computation.2 | async-start | bytes 2097152 | tf_op jit(solution)/shard_map/all_to_all | solution.py:26
  108.6 26.4 %collective-permute-start.1 = (bf16[1024,512]{1,0:T(8,128)(2,1)}, bf16[1024,512]{1,0:T(8,128)(2,1)}, u32[]{:S(2)}, u32[]{:S(2)}) collective-permute-start(bf16[1024,512]{1,0:T(8,128)(2,1)} %bitcast.5), channel_id=1, source_target_pairs={{0,16},{16,0},{1,17},{17,1},{2,18},{18,2},{3,19},{19,3},{4,20},{20... | collective-permute-start | bytes 3145736 | tf_op jit(solution)/shard_map/ppermute | solution.py:20
  110.4 46.5 %collective-permute-start.2 = (bf16[256,2048]{1,0:T(8,128)(2,1)}, bf16[256,2048]{1,0:T(8,128)(2,1)}, u32[]{:S(2)}, u32[]{:S(2)}) collective-permute-start(bf16[256,2048]{1,0:T(8,128)(2,1)} %bitcast.6), channel_id=1, source_target_pairs={{0,16},{16,0},{1,17},{17,1},{2,18},{18,2},{3,19},{19,3},{4,20},{20... | collective-permute-start | bytes 3145736 | tf_op jit(solution)/shard_map/ppermute | solution.py:20
  138.0 23.5 %copy-start.9 = (bf16[1024,512]{1,0:T(8,128)(2,1)S(1)}, bf16[1024,512]{1,0:T(8,128)(2,1)}, u32[]{:S(2)}) copy-start(bf16[1024,512]{1,0:T(8,128)(2,1)} %get-tuple-element.28) | copy-start | bytes 3145732
  138.0 23.5 %copy-start.10 = (bf16[1024,512]{1,0:T(8,128)(2,1)S(1)}, bf16[1024,512]{1,0:T(8,128)(2,1)}, u32[]{:S(2)}) copy-start(bf16[1024,512]{1,0:T(8,128)(2,1)} %get-tuple-element.29) | copy-start | bytes 3145732
  159.9 6.6 %copy-start.3 = (bf16[16,16,2048]{2,1,0:T(8,128)(2,1)}, bf16[16,16,2048]{2,1,0:T(8,128)(2,1)S(1)}, u32[]{:S(2)}) copy-start(bf16[16,16,2048]{2,1,0:T(8,128)(2,1)S(1)} %all-to-all-done.2) | copy-start | bytes 3145732
  159.9 6.6 %slice-start = ((s8[5570560]{0:T(1024)(128)(4,1)}), s8[4194304]{0:T(1024)(128)(4,1)S(1)}, s32[]{:S(2)}) async-start(s8[5570560]{0:T(1024)(128)(4,1)} %bitcast.156), calls=%async_computation.7 | async-start | bytes 8388608
  178.9 5.1 %collective-permute-start.3 = (bf16[8,80,2048]{2,1,0:T(8,128)(2,1)}, bf16[8,80,2048]{2,1,0:T(8,128)(2,1)S(1)}, u32[]{:S(2)}, u32[]{:S(2)}) collective-permute-start(bf16[8,80,2048]{2,1,0:T(8,128)(2,1)} %fusion.4), channel_id=1, source_target_pairs={{0,1},{1,0},{2,3},{3,2},{4,5},{5,4},{6,7},{7,6},{8,9},{9,8},{10,11... | collective-permute-start | bytes 7864328 | tf_op jit(solution)/shard_map/ppermute | solution.py:20
  189.8 31.0 %collective-permute-start.4 = (bf16[4,80,2048]{2,1,0:T(8,128)(2,1)S(1)}, bf16[4,80,2048]{2,1,0:T(8,128)(2,1)}, u32[]{:S(2)}, u32[]{:S(2)}) collective-permute-start(bf16[4,80,2048]{2,1,0:T(8,128)(2,1)S(1)} %fusion.18), channel_id=1, source_target_pairs={{0,2},{1,3},{2,0},{3,1},{4,6},{5,7},{6,4},{7,5},{8,10},{9,11},{10,... | collective-permute-start | bytes 3932168 | tf_op jit(solution)/shard_map/ppermute | solution.py:20
  224.2 16.3 %collective-permute-start.5 = (bf16[2,80,2048]{2,1,0:T(8,128)(2,1)}, bf16[2,80,2048]{2,1,0:T(8,128)(2,1)}, u32[]{:S(2)}, u32[]{:S(2)}) collective-permute-start(bf16[2,80,2048]{2,1,0:T(8,128)(2,1)} %fusion.24), channel_id=1, source_target_pairs={{0,4},{1,5},{2,6},{3,7},{4,0},{5,1},{6,2},{7,3},{8,12},{9,13},{10,... | collective-permute-start | bytes 1966088 | tf_op jit(solution)/shard_map/ppermute | solution.py:20
  234.6 10.9 %copy-start.16 = (s32[2,1,4]{2,1,0:T(1,128)S(1)}, s32[2,1,4]{2,1,0:T(1,128)}, u32[]{:S(2)}) copy-start(s32[2,1,4]{2,1,0:T(1,128)} %param.24) | copy-start | bytes 100
  234.6 46.6 %all-to-all-start.3 = ((bf16[16,64,512]{2,1,0:T(8,128)(2,1)}), bf16[16,64,512]{2,1,0:T(8,128)(2,1)}, u32[]{:S(2)}, u32[]{:S(2)}) async-start(bf16[16,64,512]{2,1,0:T(8,128)(2,1)} %get-tuple-element.36), calls=%async_computation.3 | async-start | bytes 2097152 | tf_op jit(solution)/shard_map/all_to_all | solution.py:31
  239.4 41.7 %copy-start.7 = (bf16[2,40,2048]{2,1,0:T(8,128)(2,1)S(1)}, bf16[2,40,2048]{2,1,0:T(8,128)(2,1)}, u32[]{:S(2)}) copy-start(bf16[2,40,2048]{2,1,0:T(8,128)(2,1)} %param.14) | copy-start | bytes 983044
  242.8 37.2 %collective-permute-start.6 = (bf16[1,80,2048]{2,1,0:T(8,128)(2,1)S(1)}, bf16[1,80,2048]{2,1,0:T(8,128)(2,1)S(1)}, u32[]{:S(2)}, u32[]{:S(2)}) collective-permute-start(bf16[1,80,2048]{2,1,0:T(8,128)(2,1)S(1)} %dynamic-slice_convert_fusion.2), channel_id=1, source_target_pairs={{0,8},{1,9},{2,10},{3,11},{4,12},{5,13},{6,14},{7,15},{8,0},{9,1},... | collective-permute-start | bytes 983048 | tf_op jit(solution)/shard_map/ppermute | solution.py:20
  245.6 62.6 %copy-start.4 = (bf16[16,16,2048]{2,1,0:T(8,128)(2,1)S(1)}, bf16[16,16,2048]{2,1,0:T(8,128)(2,1)}, u32[]{:S(2)}) copy-start(bf16[16,16,2048]{2,1,0:T(8,128)(2,1)} %copy-done.3) | copy-start | bytes 3145732
  281.2 34.8 %copy-start.8 = (bf16[2,40,2048]{2,1,0:T(8,128)(2,1)}, bf16[2,40,2048]{2,1,0:T(8,128)(2,1)S(1)}, u32[]{:S(2)}) copy-start(bf16[2,40,2048]{2,1,0:T(8,128)(2,1)S(1)} %fusion.23) | copy-start | bytes 983044
  281.2 36.6 %all-to-all-start.4 = ((bf16[16,64,512]{2,1,0:T(8,128)(2,1)}), bf16[16,64,512]{2,1,0:T(8,128)(2,1)S(1)}, u32[]{:S(2)}, u32[]{:S(2)}) async-start(bf16[16,64,512]{2,1,0:T(8,128)(2,1)} %get-tuple-element.35), calls=%async_computation.4 | async-start | bytes 2097152 | tf_op jit(solution)/shard_map/all_to_all | solution.py:31
  285.3 1.3 collective-permute-start.7
  286.6 7.6 %collective-permute-start.8 = (bf16[2,4,2048]{2,1,0:T(4,128)(2,1)S(1)}, bf16[2,4,2048]{2,1,0:T(4,128)(2,1)S(1)}, u32[]{:S(2)}, u32[]{:S(2)}) collective-permute-start(bf16[2,4,2048]{2,1,0:T(4,128)(2,1)S(1)} %add.207), channel_id=1, source_target_pairs={{0,2},{1,3},{2,0},{3,1},{4,6},{5,7},{6,4},{7,5},{8,10},{9,11},{10,... | collective-permute-start | bytes 98312 | tf_op jit(solution)/shard_map/ppermute | solution.py:20
  294.2 9.4 %collective-permute-start.9 = (bf16[2,4,2048]{2,1,0:T(4,128)(2,1)S(1)}, bf16[2,4,2048]{2,1,0:T(4,128)(2,1)S(1)}, u32[]{:S(2)}, u32[]{:S(2)}) collective-permute-start(bf16[2,4,2048]{2,1,0:T(4,128)(2,1)S(1)} %add.208), channel_id=1, source_target_pairs={{0,4},{1,5},{2,6},{3,7},{4,0},{5,1},{6,2},{7,3},{8,12},{9,13},{10,... | collective-permute-start | bytes 98312 | tf_op jit(solution)/shard_map/ppermute | solution.py:20
  303.7 9.2 %collective-permute-start.10 = (bf16[2,4,2048]{2,1,0:T(4,128)(2,1)S(1)}, bf16[2,4,2048]{2,1,0:T(4,128)(2,1)S(1)}, u32[]{:S(2)}, u32[]{:S(2)}) collective-permute-start(bf16[2,4,2048]{2,1,0:T(4,128)(2,1)S(1)} %add.209), channel_id=1, source_target_pairs={{0,8},{1,9},{2,10},{3,11},{4,12},{5,13},{6,14},{7,15},{8,0},{9,1},... | collective-permute-start | bytes 98312 | tf_op jit(solution)/shard_map/ppermute | solution.py:20
  308.9 12.7 %copy-start.15 = (f32[2048]{0:T(1024)S(1)}, f32[2048]{0:T(1024)}, u32[]{:S(2)}) copy-start(f32[2048]{0:T(1024)} %param.18) | copy-start | bytes 24580
  313.1 4.3 %collective-permute-start.11 = (bf16[2,2,4,2048]{3,2,1,0:T(4,128)(2,1)S(1)}, bf16[2,2,4,2048]{3,2,1,0:T(4,128)(2,1)S(1)}, u32[]{:S(2)}, u32[]{:S(2)}) collective-permute-start(bf16[2,2,4,2048]{3,2,1,0:T(4,128)(2,1)S(1)} %broadcast_select_fusion.9), channel_id=1, source_target_pairs={{0,16},{16,0},{1,17},{17,1},{2,18},{18,2},{3,19},{19,3},{4,20},{20... | collective-permute-start | bytes 196616 | tf_op jit(solution)/shard_map/ppermute | solution.py:20
  317.9 32.2 %all-to-all-start.5 = ((bf16[16,16,2048]{2,1,0:T(8,128)(2,1)}), bf16[16,16,2048]{2,1,0:T(8,128)(2,1)S(1)}, u32[]{:S(2)}, u32[]{:S(2)}) async-start(bf16[16,16,2048]{2,1,0:T(8,128)(2,1)} %broadcast_select_fusion.2), calls=%async_computation.5 | async-start | bytes 2097152 | tf_op jit(solution)/shard_map/all_to_all | solution.py:31
  325.7 1.3 collective-permute-start.12
  327.0 3.6 %collective-permute-start.13 = (f32[2,16]{1,0:T(2,128)S(1)}, f32[2,16]{1,0:T(2,128)S(1)}, u32[]{:S(2)}, u32[]{:S(2)}) collective-permute-start(f32[2,16]{1,0:T(2,128)S(1)} %pad_maximum_fusion.2), channel_id=1, source_target_pairs={{0,2},{1,3},{2,0},{3,1},{4,6},{5,7},{6,4},{7,5},{8,10},{9,11},{10,... | collective-permute-start | bytes 392 | tf_op jit(solution)/shard_map/ppermute | solution.py:20
  330.7 9.1 %collective-permute-start.14 = (f32[2,16]{1,0:T(2,128)S(1)}, f32[2,16]{1,0:T(2,128)S(1)}, u32[]{:S(2)}, u32[]{:S(2)}) collective-permute-start(f32[2,16]{1,0:T(2,128)S(1)} %pad_maximum_fusion.3), channel_id=1, source_target_pairs={{0,4},{1,5},{2,6},{3,7},{4,0},{5,1},{6,2},{7,3},{8,12},{9,13},{10,... | collective-permute-start | bytes 392 | tf_op jit(solution)/shard_map/ppermute | solution.py:20
  339.8 8.4 %collective-permute-start.15 = (f32[2,16]{1,0:T(2,128)S(1)}, f32[2,16]{1,0:T(2,128)S(1)}, u32[]{:S(2)}, u32[]{:S(2)}) collective-permute-start(f32[2,16]{1,0:T(2,128)S(1)} %pad_maximum_fusion.4), channel_id=1, source_target_pairs={{0,8},{1,9},{2,10},{3,11},{4,12},{5,13},{6,14},{7,15},{8,0},{9,1},... | collective-permute-start | bytes 392 | tf_op jit(solution)/shard_map/ppermute | solution.py:20
  348.2 3.6 collective-permute-start.16
  (12 other events, 42.9 us)
Sparse Core Ops, SparseCore 0:
  11.5 92.1 all-gather.1

commit v3 on v2

--- a/solution.py
+++ b/solution.py
@@ -1,7 +1,13 @@
+import functools
+
 import jax
 import jax.numpy as jnp
 from jax import lax
+from jax.experimental import pallas as pl
+from jax.experimental.pallas import tpu as pltpu
 from jax.sharding import PartitionSpec as P
+
+MESH = pl.DeviceIdType.MESH
 
 
 def normalize(rows, gain):
@@ -66,18 +72,86 @@
     return held[0]
 
 
-def butterfly(value, axis, join):
-    bit = 1
-    while bit < lax.axis_size(axis):
-        value = join(value, exchange(value, axis, bit))
-        bit *= 2
-    return value
-
-
-def join_stats(ours, theirs):
-    top = jnp.maximum(ours[0], theirs[0])
-    total = ours[1] * jnp.exp(ours[0] - top) + theirs[1] * jnp.exp(theirs[0] - top)
-    return jnp.stack([top, total])
+def bits_of(size):
+    bits = []
+    while 2 ** len(bits) < size:
+        bits.append(2 ** len(bits))
+    return bits
+
+
+def tail_kernel(
+    ep_bits, grp_bits, tails_ref, gain_ref, head_ref, out_ref, held, came, stat, stat_came,
+    send_sem, recv_sem,
+):
+    grp, ep = lax.axis_index("grp"), lax.axis_index("ep")
+    partners = [(grp, ep + bit * (1 - 2 * ((ep // bit) % 2))) for bit in ep_bits]
+    partners += [(grp + bit * (1 - 2 * ((grp // bit) % 2)), ep) for bit in grp_bits]
+    rounds = len(partners)
+    barrier = pltpu.get_barrier_semaphore()
+    for partner in partners:
+        pl.semaphore_signal(barrier, inc=1, device_id=partner, device_id_type=MESH)
+    pl.semaphore_wait(barrier, rounds)
+
+    def swap(source, target, slot, partner):
+        copy = pltpu.make_async_remote_copy(
+            src_ref=source,
+            dst_ref=target,
+            send_sem=send_sem.at[slot],
+            recv_sem=recv_sem.at[slot],
+            device_id=partner,
+            device_id_type=MESH,
+        )
+        copy.start()
+        copy.wait()
+
+    held[0] = tails_ref[...]
+    for step, partner in enumerate(partners):
+        swap(held.at[step], came.at[step], step, partner)
+        both = held[step].astype(jnp.float32) + came[step].astype(jnp.float32)
+        held[step + 1] = both.astype(jnp.bfloat16)
+    rows = held[rounds].astype(jnp.float32)
+    scale = lax.rsqrt(jnp.mean(rows * rows, axis=-1, keepdims=True) + 1e-06)
+    finals = (rows * scale * gain_ref[...]).astype(jnp.bfloat16)
+    out_ref[...] = jnp.dot(finals, head_ref[...], preferred_element_type=jnp.float32)
+    logits = out_ref[...]
+    top = jnp.max(logits, axis=1, keepdims=True)
+    total = jnp.sum(jnp.exp(logits - top), axis=1, keepdims=True)
+    lanes = stat.shape[2:]
+    stat[0, 0] = jnp.broadcast_to(top, lanes)
+    stat[0, 1] = jnp.broadcast_to(total, lanes)
+    for step, partner in enumerate(partners):
+        swap(stat.at[step], stat_came.at[step], rounds + step, partner)
+        ours, theirs = stat[step, 0], stat_came[step, 0]
+        top = jnp.maximum(ours, theirs)
+        stat[step + 1, 0] = top
+        stat[step + 1, 1] = stat[step, 1] * jnp.exp(ours - top) + stat_came[step, 1] * jnp.exp(
+            theirs - top
+        )
+    shift = stat[rounds, 0] + jnp.log(stat[rounds, 1])
+    out_ref[...] = out_ref[...] - shift[:, :1]
+
+
+def tail_probs(tails, gain, head):
+    ep_bits, grp_bits = bits_of(lax.axis_size("ep")), bits_of(lax.axis_size("grp"))
+    rounds = len(ep_bits) + len(grp_bits)
+    count, width = tails.shape
+    return pl.pallas_call(
+        functools.partial(tail_kernel, ep_bits, grp_bits),
+        out_shape=jax.ShapeDtypeStruct((count, head.shape[1]), jnp.float32),
+        in_specs=[pl.BlockSpec(memory_space=pltpu.VMEM)] * 3,
+        out_specs=pl.BlockSpec(memory_space=pltpu.VMEM),
+        scratch_shapes=[
+            pltpu.VMEM((rounds + 1, count, width), jnp.bfloat16),
+            pltpu.VMEM((rounds, count, width), jnp.bfloat16),
+            pltpu.VMEM((rounds + 1, 2, count, 128), jnp.float32),
+            pltpu.VMEM((rounds, 2, count, 128), jnp.float32),
+            pltpu.SemaphoreType.DMA((2 * rounds,)),
+            pltpu.SemaphoreType.DMA((2 * rounds,)),
+        ],
+        compiler_params=pltpu.CompilerParams(
+            collective_id=0, has_side_effects=True, vmem_limit_bytes=40 * 2**20
+        ),
+    )(tails, gain[None, :], head)
 
 
 def per_device(
@@ -116,7 +190,9 @@
     gate_full = gather_rows(gate_proj[0], "grp")
     up_full = gather_rows(up_proj[0], "grp")
     down_full = gather_rows(down_proj[0], "grp")
-    spread = tuple(spread_rows(weights) for weights in (gate_proj, up_proj, down_proj))
+    up_next, gate_full = lax.optimization_barrier((up_proj, gate_full))
+    down_next, up_full = lax.optimization_barrier((down_proj, up_full))
+    spread = tuple(spread_rows(weights) for weights in (gate_proj, up_next, down_next))
     rows, spread = lax.optimization_barrier((rows, spread))
 
     tokens = rows[:, :width]
@@ -145,21 +221,10 @@
     tails = jnp.einsum(
         "brt,btd->brd", picker, mixed, preferred_element_type=jnp.float32
     ).astype(jnp.bfloat16)
-    add = lambda a, b: a + b
-    tails = butterfly(tails, "ep", add)
     here = (jnp.arange(n_grp, dtype=jnp.int32) == group)[None, :, None, None]
     placed = jnp.where(here, tails[:, None], jnp.zeros((), jnp.bfloat16))
-    placed = butterfly(placed, "grp", add)
-    finals = normalize(placed.reshape(-1, width).astype(jnp.float32), final_gain)
-    logits = jnp.dot(finals, head_proj, preferred_element_type=jnp.float32)
-    top = jnp.max(logits, axis=1)
-    total = jnp.sum(jnp.exp(logits - top[:, None]), axis=1)
-    stats = jnp.stack([top, total])
-    stats = butterfly(stats, "ep", join_stats)
-    stats = butterfly(stats, "grp", join_stats)
-    log_probs = (logits - stats[0][:, None] - jnp.log(stats[1])[:, None]).reshape(
-        batches, -1, logits.shape[1]
-    )
+    log_probs = tail_probs(placed.reshape(-1, width), final_gain, head_proj)
+    log_probs = log_probs.reshape(batches, -1, log_probs.shape[1])
     return (mixed, *moved, log_probs)
 
 

time: 365 us -> 342 us (0.937)
  blocking collectives: 43.3 us -> 0 us
  Pallas kernels: 0 us -> 30.7 us
  waiting for transfers between devices: 186 us -> 175 us
  matrix products: 15.3 us -> 19.2 us
    all_to_all x1 -> x0, blocking collectives: 43.3 us -> none  [spread_rows(): return lax.all_to_all(rows, 'ep', split_axis=0, concat_axis=0, tiled=True)]
    all_to_all x3, waiting for transfers between devices: 0.01 us -> 34.5 us  [relocate(): lax.all_to_all(ordered, 'ep', split_axis=0, concat_axis=0, tiled=True)]
    pallas_call x0 -> x1, Pallas kernels: none -> 30.7 us  [tail_probs(): pl.pallas_call(functools.partial(tail_kernel, ep_bits, grp_bits), out_sha...]
    ppermute x17 -> x7, waiting for transfers between devices: 148 us -> 122 us  [exchange(): return lax.ppermute(value, axis, [(i, i ^ bit) for i in range(n)])]
    all_to_all x2 -> x3, waiting for transfers between devices: 38.3 us -> 18.1 us  [spread_rows(): return lax.all_to_all(rows, 'ep', split_axis=0, concat_axis=0, tiled=True)]
    ppermute x17 -> x7, starting transfers between devices: 28.8 us -> 11.3 us  [exchange(): return lax.ppermute(value, axis, [(i, i ^ bit) for i in range(n)])]
    all_to_all x2 -> x3, starting transfers between devices: 13 us -> 23.5 us  [spread_rows(): return lax.all_to_all(rows, 'ep', split_axis=0, concat_axis=0, tiled=True)]
    dot_general x1, matrix products: 2.9 us -> 11.4 us  [per_device(): outputs = jnp.dot(hidden, down_full, preferred_element_type=jnp.float32)]
  transfers between devices with their start and end apart: 23 -> 14, of which waited for: 17 -> 10; matrix products, arithmetic and copies ran while one was open for 7% -> 7% of each run, Pallas kernels for 0% -> 0%
where the time goes in v3:
time: 342 us; the launch traced here: 341 us
  waiting for transfers between devices  175 us (51%)
  starting transfers between devices  54.5 us (16%)
  Pallas kernels  30.7 us (9%)
  other arithmetic  24.4 us (7%)
  local copies, waits for them, and re-layouts  22.6 us (7%)
  matrix products  19.2 us (6%)
  between operations  14.4 us (4%)
    ppermute x7, waiting for transfers between devices, exchange(): return lax.ppermute(value, axis, [(i, i ^ bit) for i in range(n)])  122 us
    all_to_all x3, waiting for transfers between devices, relocate(): lax.all_to_all(ordered, 'ep', split_axis=0, concat_axis=0, tiled=True)  34.5 us
    pallas_call x1, Pallas kernels, tail_probs(): pl.pallas_call(functools.partial(tail_kernel, ep_bits, grp_bits), out_sha...  30.7 us
    all_to_all x3, starting transfers between devices, spread_rows(): return lax.all_to_all(rows, 'ep', split_axis=0, concat_axis=0, tiled=True)  23.5 us
    all_to_all x3, starting transfers between devices, relocate(): lax.all_to_all(ordered, 'ep', split_axis=0, concat_axis=0, tiled=True)  19.7 us
    all_to_all x3, waiting for transfers between devices, spread_rows(): return lax.all_to_all(rows, 'ep', split_axis=0, concat_axis=0, tiled=True)  18.1 us
    unnamed x35, local copies, waits for them, and re-layouts  11.8 us
    dot_general x1, matrix products, per_device(): outputs = jnp.dot(hidden, down_full, preferred_element_type=jnp.float32)  11.4 us
  transfers between devices with their start and end apart: 14, of which 10 were waited for; matrix products, arithmetic and copies ran while one was open for 7% of the time, Pallas kernels for 0%

profile of v3, /device:TPU:0, one launch (start us, length us, event | category | flops | bytes accessed | tf_op | source)
XLA Modules:
  0.0 340.9 jit_solution(17453706040253694007)
XLA Ops:
  11.3 7.4 %all-to-all-start = ((bf16[16,64,512]{2,1,0:T(8,128)(2,1)}), bf16[16,64,512]{2,1,0:T(8,128)(2,1)S(1)}, u32[]{:S(2)}, u32[]{:S(2)}) async-start(bf16[16,64,512]{2,1,0:T(8,128)(2,1)} %bitcast.52), calls=%async_computation | async-start | bytes 2097152 | tf_op jit(solution)/shard_map/all_to_all | solution.py:32
  20.3 24.1 %collective-permute-done.1 = bf16[1024,512]{1,0:T(8,128)(2,1)S(1)} collective-permute-done((bf16[1024,512]{1,0:T(8,128)(2,1)}, bf16[1024,512]{1,0:T(8,128)(2,1)S(1)}, u32[]{:S(2)}, u32[]{:S(2)}) %collective-permute-start.1) | collective-permute-done | bytes 1048608 | tf_op jit(solution)/shard_map/ppermute | solution.py:26
  47.2 5.5 %all-to-all-done = bf16[16,64,512]{2,1,0:T(8,128)(2,1)S(1)} async-done(((bf16[16,64,512]{2,1,0:T(8,128)(2,1)}), bf16[16,64,512]{2,1,0:T(8,128)(2,1)S(1)}, u32[]{:S(2)}, u32[]{:S(2)}) %all-to-all-start) | async-done | bytes 1048608 | tf_op jit(solution)/shard_map/all_to_all | solution.py:32
  52.7 7.0 %all-to-all-start.2 = ((bf16[16,16,2048]{2,1,0:T(8,128)(2,1)}), bf16[16,16,2048]{2,1,0:T(8,128)(2,1)S(1)}, u32[]{:S(2)}, u32[]{:S(2)}) async-start(bf16[16,16,2048]{2,1,0:T(8,128)(2,1)} %bitcast.5), calls=%async_computation.2 | async-start | bytes 2097152 | tf_op jit(solution)/shard_map/all_to_all | solution.py:32
  61.2 24.0 %collective-permute-done = bf16[1024,512]{1,0:T(8,128)(2,1)S(1)} collective-permute-done((bf16[1024,512]{1,0:T(8,128)(2,1)S(1)}, bf16[1024,512]{1,0:T(8,128)(2,1)S(1)}, u32[]{:S(2)}, u32[]{:S(2)}) %collective-permute-start) | collective-permute-done | bytes 1048608 | tf_op jit(solution)/shard_map/ppermute | solution.py:26
  86.9 12.7 %all-to-all-done.2 = bf16[16,16,2048]{2,1,0:T(8,128)(2,1)S(1)} async-done(((bf16[16,16,2048]{2,1,0:T(8,128)(2,1)}), bf16[16,16,2048]{2,1,0:T(8,128)(2,1)S(1)}, u32[]{:S(2)}, u32[]{:S(2)}) %all-to-all-start.2) | async-done | bytes 1048608 | tf_op jit(solution)/shard_map/all_to_all | solution.py:32
  99.6 9.1 %all-to-all-start.1 = ((bf16[16,64,512]{2,1,0:T(8,128)(2,1)}), bf16[16,64,512]{2,1,0:T(8,128)(2,1)}, u32[]{:S(2)}, u32[]{:S(2)}) async-start(bf16[16,64,512]{2,1,0:T(8,128)(2,1)} %bitcast.3), calls=%async_computation.1 | async-start | bytes 2097152 | tf_op jit(solution)/shard_map/all_to_all | solution.py:32
  108.7 1.8 collective-permute-start.2
  111.4 23.0 %collective-permute-done.2 = bf16[256,2048]{1,0:T(8,128)(2,1)S(1)} collective-permute-done((bf16[256,2048]{1,0:T(8,128)(2,1)}, bf16[256,2048]{1,0:T(8,128)(2,1)S(1)}, u32[]{:S(2)}, u32[]{:S(2)}) %collective-permute-start.2) | collective-permute-done | bytes 1048608 | tf_op jit(solution)/shard_map/ppermute | solution.py:26
  134.4 2.8 broadcast_select_fusion.4
  137.2 7.6 %fusion.2 = f32[1280,512]{1,0:T(8,128)} fusion(bf16[2048,512]{1,0:T(8,128)(2,1)} %pad_maximum_fusion, bf16[1280,2176]{1,0:T(8,128)(2,1)} %all-gather.2.cloned.1.call-done), kind=kOutput, calls=%fused_computation.9 | convolution fusion | flops 2684354560 | bytes 9961472 | tf_op jit(solution)/shard_map/dot_general | solution.py:203
  145.9 11.4 %convolution_multiply_fusion = f32[1280,2048]{1,0:T(8,128)} fusion(f32[1280]{0:T(1024)S(1)} %select_reduce_fusion, bf16[256,2048]{1,0:T(8,128)(2,1)} %get-tuple-element.25, bf16[256,2048]{1,0:T(8,128)(2,1)S(1)} %copy-done.11, bf16[2048,512]{1,0:T(8,128)(2,1)} %pad_maximum_fusion.1, bf16[1280,2176]{1,0:T(8,128)(2,1)} %all-gather.2.cloned.1.call-done, ...), kind=kOutput, calls=%fused_computation.4 | convolution fusion | flops 5379457024 | bytes 22549504 | tf_op jit(solution)/shard_map/dot_general | solution.py:206
  157.3 4.4 %fusion.10 = bf16[8,80,2048]{2,1,0:T(8,128)(2,1)} fusion(f32[8,2,80,2048]{3,2,1,0:T(8,128)} %bitcast.50, s32[]{:T(128)S(6)} %select_n.165), kind=kLoop, calls=%fused_computation.13 | loop fusion | bytes 5242884 | tf_op jit(solution)/shard_map/convert_element_type | solution.py:70
  162.3 1.8 gather_fusion.3
  164.2 1.6 broadcast_select_fusion
  165.8 5.9 %all-to-all-start.3 = ((bf16[16,64,512]{2,1,0:T(8,128)(2,1)}), bf16[16,64,512]{2,1,0:T(8,128)(2,1)S(1)}, u32[]{:S(2)}, u32[]{:S(2)}) async-start(bf16[16,64,512]{2,1,0:T(8,128)(2,1)} %get-tuple-element.34), calls=%async_computation.3 | async-start | bytes 2097152 | tf_op jit(solution)/shard_map/all_to_all | solution.py:37
  171.7 22.9 %all-to-all-done.3 = bf16[16,64,512]{2,1,0:T(8,128)(2,1)S(1)} async-done(((bf16[16,64,512]{2,1,0:T(8,128)(2,1)}), bf16[16,64,512]{2,1,0:T(8,128)(2,1)S(1)}, u32[]{:S(2)}, u32[]{:S(2)}) %all-to-all-start.3) | async-done | bytes 1048608 | tf_op jit(solution)/shard_map/all_to_all | solution.py:37
  194.6 6.9 %all-to-all-start.4 = ((bf16[16,64,512]{2,1,0:T(8,128)(2,1)}), bf16[16,64,512]{2,1,0:T(8,128)(2,1)S(1)}, u32[]{:S(2)}, u32[]{:S(2)}) async-start(bf16[16,64,512]{2,1,0:T(8,128)(2,1)} %get-tuple-element.33), calls=%async_computation.4 | async-start | bytes 2097152 | tf_op jit(solution)/shard_map/all_to_all | solution.py:37
  201.5 4.1 %bitcast_add_fusion = f32[8,80,2048]{2,1,0:T(8,128)S(1)} fusion(bf16[8,80,2048]{2,1,0:T(8,128)(2,1)} %collective-permute-done.3, f32[8,2,80,2048]{3,2,1,0:T(8,128)} %bitcast.51, s32[]{:T(128)S(6)} %select_n.164), kind=kLoop, calls=%fused_computation.6 | loop fusion | flops 2621440 | bytes 13107204 | tf_op jit(solution)/shard_map/add | solution.py:70
  205.6 2.3 copy-done.2
  209.2 1.9 collective-permute-start.4
  212.9 11.6 %all-to-all-done.4 = bf16[16,64,512]{2,1,0:T(8,128)(2,1)S(1)} async-done(((bf16[16,64,512]{2,1,0:T(8,128)(2,1)}), bf16[16,64,512]{2,1,0:T(8,128)(2,1)S(1)}, u32[]{:S(2)}, u32[]{:S(2)}) %all-to-all-start.4) | async-done | bytes 1048608 | tf_op jit(solution)/shard_map/all_to_all | solution.py:37
  224.5 7.0 %all-to-all-start.5 = ((bf16[16,16,2048]{2,1,0:T(8,128)(2,1)}), bf16[16,16,2048]{2,1,0:T(8,128)(2,1)}, u32[]{:S(2)}, u32[]{:S(2)}) async-start(bf16[16,16,2048]{2,1,0:T(8,128)(2,1)} %broadcast_select_fusion.2), calls=%async_computation.5 | async-start | bytes 2097152 | tf_op jit(solution)/shard_map/all_to_all | solution.py:37
  231.5 21.1 %collective-permute-done.4 = bf16[4,80,2048]{2,1,0:T(8,128)(2,1)} collective-permute-done((bf16[4,80,2048]{2,1,0:T(8,128)(2,1)}, bf16[4,80,2048]{2,1,0:T(8,128)(2,1)}, u32[]{:S(2)}, u32[]{:S(2)}) %collective-permute-start.4) | collective-permute-done | bytes 1310752 | tf_op jit(solution)/shard_map/ppermute | solution.py:26
  252.5 2.4 bitcast_add_fusion.1
  255.9 2.9 collective-permute-start.5
  259.0 15.0 %collective-permute-done.5 = bf16[2,80,2048]{2,1,0:T(8,128)(2,1)} collective-permute-done((bf16[2,80,2048]{2,1,0:T(8,128)(2,1)}, bf16[2,80,2048]{2,1,0:T(8,128)(2,1)}, u32[]{:S(2)}, u32[]{:S(2)}) %collective-permute-start.5) | collective-permute-done | bytes 655392 | tf_op jit(solution)/shard_map/ppermute | solution.py:26
  276.3 1.6 collective-permute-start.6
  278.1 15.3 %collective-permute-done.6 = bf16[1,80,2048]{2,1,0:T(8,128)(2,1)S(1)} collective-permute-done((bf16[1,80,2048]{2,1,0:T(8,128)(2,1)S(1)}, bf16[1,80,2048]{2,1,0:T(8,128)(2,1)S(1)}, u32[]{:S(2)}, u32[]{:S(2)}) %collective-permute-start.6) | collective-permute-done | bytes 327712 | tf_op jit(solution)/shard_map/ppermute | solution.py:26
  295.0 2.8 copy-done
  297.8 30.7 %shard_map.155 = f32[16,1536]{1,0:T(8,128)S(1)} custom-call(bf16[16,2048]{1,0:T(8,128)(2,1)S(1)} %broadcast_select_fusion.9.tails_ref, f32[1,2048]{1,0:T(1,128)S(1)} %bitcast.45, bf16[2048,1536]{1,0:T(8,128)(2,1)S(1)} %copy-done), custom_call_target="tpu_custom_call" | custom-call | tf_op jit(solution)/shard_map/pallas_call | solution.py:138
  331.1 2.3 copy.36
  (82 shorter events, 25.8 us)
Async XLA Ops:
  7.2 130.0 %all-gather.2.cloned.1.call-start = ((), (), s32[]{:S(2)}) async-start(), calls=%async_computation.6 | async-start | bytes 5918720 | tf_op jit(solution)/shard_map/all_gather | solution.py:187
  11.3 41.4 %all-to-all-start = ((bf16[16,64,512]{2,1,0:T(8,128)(2,1)}), bf16[16,64,512]{2,1,0:T(8,128)(2,1)S(1)}, u32[]{:S(2)}, u32[]{:S(2)}) async-start(bf16[16,64,512]{2,1,0:T(8,128)(2,1)} %bitcast.52), calls=%async_computation | async-start | bytes 2097152 | tf_op jit(solution)/shard_map/all_to_all | solution.py:32
  18.7 25.7 %collective-permute-start.1 = (bf16[1024,512]{1,0:T(8,128)(2,1)}, bf16[1024,512]{1,0:T(8,128)(2,1)S(1)}, u32[]{:S(2)}, u32[]{:S(2)}) collective-permute-start(bf16[1024,512]{1,0:T(8,128)(2,1)} %bitcast.4), channel_id=1, source_target_pairs={{0,16},{16,0},{1,17},{17,1},{2,18},{18,2},{3,19},{19,3},{4,20},{20... | collective-permute-start | bytes 3145736 | tf_op jit(solution)/shard_map/ppermute | solution.py:26
  45.8 13.9 %copy-start.3 = (bf16[1,1024,512]{2,1,0:T(8,128)(2,1)S(1)}, bf16[1,1024,512]{2,1,0:T(8,128)(2,1)}, u32[]{:S(2)}) copy-start(bf16[1,1024,512]{2,1,0:T(8,128)(2,1)} %param.19) | copy-start | bytes 3145732
  52.7 46.9 %all-to-all-start.2 = ((bf16[16,16,2048]{2,1,0:T(8,128)(2,1)}), bf16[16,16,2048]{2,1,0:T(8,128)(2,1)S(1)}, u32[]{:S(2)}, u32[]{:S(2)}) async-start(bf16[16,16,2048]{2,1,0:T(8,128)(2,1)} %bitcast.5), calls=%async_computation.2 | async-start | bytes 2097152 | tf_op jit(solution)/shard_map/all_to_all | solution.py:32
  59.7 25.6 %collective-permute-start = (bf16[1024,512]{1,0:T(8,128)(2,1)S(1)}, bf16[1024,512]{1,0:T(8,128)(2,1)S(1)}, u32[]{:S(2)}, u32[]{:S(2)}) collective-permute-start(bf16[1024,512]{1,0:T(8,128)(2,1)S(1)} %bitcast.53), channel_id=1, source_target_pairs={{0,16},{16,0},{1,17},{17,1},{2,18},{18,2},{3,19},{19,3},{4,20},{20... | collective-permute-start | bytes 3145736 | tf_op jit(solution)/shard_map/ppermute | solution.py:26
  85.4 25.2 %copy-start.14 = (s32[16]{0:T(128)S(1)}, s32[16]{0:T(128)}, u32[]{:S(2)}) copy-start(s32[16]{0:T(128)} %param.23) | copy-start | bytes 196
  85.4 25.2 %copy-start.13 = (s32[16]{0:T(128)S(1)}, s32[16]{0:T(128)}, u32[]{:S(2)}) copy-start(s32[16]{0:T(128)} %param.22) | copy-start | bytes 196
  99.6 37.6 %all-to-all-start.1 = ((bf16[16,64,512]{2,1,0:T(8,128)(2,1)}), bf16[16,64,512]{2,1,0:T(8,128)(2,1)}, u32[]{:S(2)}, u32[]{:S(2)}) async-start(bf16[16,64,512]{2,1,0:T(8,128)(2,1)} %bitcast.3), calls=%async_computation.1 | async-start | bytes 2097152 | tf_op jit(solution)/shard_map/all_to_all | solution.py:32
  108.7 25.6 %collective-permute-start.2 = (bf16[256,2048]{1,0:T(8,128)(2,1)}, bf16[256,2048]{1,0:T(8,128)(2,1)S(1)}, u32[]{:S(2)}, u32[]{:S(2)}) collective-permute-start(bf16[256,2048]{1,0:T(8,128)(2,1)} %bitcast.6), channel_id=1, source_target_pairs={{0,16},{16,0},{1,17},{17,1},{2,18},{18,2},{3,19},{19,3},{4,20},{20... | collective-permute-start | bytes 3145736 | tf_op jit(solution)/shard_map/ppermute | solution.py:26
  137.2 8.8 %copy-start.11 = (bf16[256,2048]{1,0:T(8,128)(2,1)S(1)}, bf16[256,2048]{1,0:T(8,128)(2,1)}, u32[]{:S(2)}) copy-start(bf16[256,2048]{1,0:T(8,128)(2,1)} %get-tuple-element.24) | copy-start | bytes 3145732
  161.7 39.8 %collective-permute-start.3 = (bf16[8,80,2048]{2,1,0:T(8,128)(2,1)}, bf16[8,80,2048]{2,1,0:T(8,128)(2,1)}, u32[]{:S(2)}, u32[]{:S(2)}) collective-permute-start(bf16[8,80,2048]{2,1,0:T(8,128)(2,1)} %fusion.10), channel_id=1, source_target_pairs={{0,1},{1,0},{2,3},{3,2},{4,5},{5,4},{6,7},{7,6},{8,9},{9,8},{10,11... | collective-permute-start | bytes 7864328 | tf_op jit(solution)/shard_map/ppermute | solution.py:26
  165.8 28.8 %all-to-all-start.3 = ((bf16[16,64,512]{2,1,0:T(8,128)(2,1)}), bf16[16,64,512]{2,1,0:T(8,128)(2,1)S(1)}, u32[]{:S(2)}, u32[]{:S(2)}) async-start(bf16[16,64,512]{2,1,0:T(8,128)(2,1)} %get-tuple-element.34), calls=%async_computation.3 | async-start | bytes 2097152 | tf_op jit(solution)/shard_map/all_to_all | solution.py:37
  194.6 11.0 %copy-start.4 = (bf16[16,64,512]{2,1,0:T(8,128)(2,1)}, bf16[16,64,512]{2,1,0:T(8,128)(2,1)S(1)}, u32[]{:S(2)}) copy-start(bf16[16,64,512]{2,1,0:T(8,128)(2,1)S(1)} %all-to-all-done.3) | copy-start | bytes 3145732
  194.6 29.9 %all-to-all-start.4 = ((bf16[16,64,512]{2,1,0:T(8,128)(2,1)}), bf16[16,64,512]{2,1,0:T(8,128)(2,1)S(1)}, u32[]{:S(2)}, u32[]{:S(2)}) async-start(bf16[16,64,512]{2,1,0:T(8,128)(2,1)} %get-tuple-element.33), calls=%async_computation.4 | async-start | bytes 2097152 | tf_op jit(solution)/shard_map/all_to_all | solution.py:37
  205.6 2.3 copy-start.2
  209.2 43.3 %collective-permute-start.4 = (bf16[4,80,2048]{2,1,0:T(8,128)(2,1)}, bf16[4,80,2048]{2,1,0:T(8,128)(2,1)}, u32[]{:S(2)}, u32[]{:S(2)}) collective-permute-start(bf16[4,80,2048]{2,1,0:T(8,128)(2,1)} %fusion.14), channel_id=1, source_target_pairs={{0,2},{1,3},{2,0},{3,1},{4,6},{5,7},{6,4},{7,5},{8,10},{9,11},{10,... | collective-permute-start | bytes 3932168 | tf_op jit(solution)/shard_map/ppermute | solution.py:26
  224.5 7.0 %copy-start.6 = (bf16[16,64,512]{2,1,0:T(8,128)(2,1)}, bf16[16,64,512]{2,1,0:T(8,128)(2,1)S(1)}, u32[]{:S(2)}) copy-start(bf16[16,64,512]{2,1,0:T(8,128)(2,1)S(1)} %all-to-all-done.4) | copy-start | bytes 3145732
  224.5 53.6 %all-to-all-start.5 = ((bf16[16,16,2048]{2,1,0:T(8,128)(2,1)}), bf16[16,16,2048]{2,1,0:T(8,128)(2,1)}, u32[]{:S(2)}, u32[]{:S(2)}) async-start(bf16[16,16,2048]{2,1,0:T(8,128)(2,1)} %broadcast_select_fusion.2), calls=%async_computation.5 | async-start | bytes 2097152 | tf_op jit(solution)/shard_map/all_to_all | solution.py:37
  231.4 27.4 %copy-start.12 = (s32[2,1,4]{2,1,0:T(1,128)S(1)}, s32[2,1,4]{2,1,0:T(1,128)}, u32[]{:S(2)}) copy-start(s32[2,1,4]{2,1,0:T(1,128)} %param.24) | copy-start | bytes 100
  255.9 18.1 %collective-permute-start.5 = (bf16[2,80,2048]{2,1,0:T(8,128)(2,1)}, bf16[2,80,2048]{2,1,0:T(8,128)(2,1)}, u32[]{:S(2)}, u32[]{:S(2)}) collective-permute-start(bf16[2,80,2048]{2,1,0:T(8,128)(2,1)} %fusion.22), channel_id=1, source_target_pairs={{0,4},{1,5},{2,6},{3,7},{4,0},{5,1},{6,2},{7,3},{8,12},{9,13},{10,... | collective-permute-start | bytes 1966088 | tf_op jit(solution)/shard_map/ppermute | solution.py:26
  259.0 35.6 %copy-start.9 = (bf16[2,40,2048]{2,1,0:T(8,128)(2,1)S(1)}, bf16[2,40,2048]{2,1,0:T(8,128)(2,1)}, u32[]{:S(2)}) copy-start(bf16[2,40,2048]{2,1,0:T(8,128)(2,1)} %param.14) | copy-start | bytes 983044
  275.2 1.1 copy-start.8
  276.3 18.7 %copy-start.1 = (f32[2048]{0:T(1024)S(1)}, f32[2048]{0:T(1024)}, u32[]{:S(2)}) copy-start(f32[2048]{0:T(1024)} %param.18) | copy-start | bytes 24580
  276.3 17.0 %collective-permute-start.6 = (bf16[1,80,2048]{2,1,0:T(8,128)(2,1)S(1)}, bf16[1,80,2048]{2,1,0:T(8,128)(2,1)S(1)}, u32[]{:S(2)}, u32[]{:S(2)}) collective-permute-start(bf16[1,80,2048]{2,1,0:T(8,128)(2,1)S(1)} %dynamic-slice_convert_fusion.2), channel_id=1, source_target_pairs={{0,8},{1,9},{2,10},{3,11},{4,12},{5,13},{6,14},{7,15},{8,0},{9,1},... | collective-permute-start | bytes 983048 | tf_op jit(solution)/shard_map/ppermute | solution.py:26
  294.6 33.9 %copy-start.10 = (bf16[2,40,2048]{2,1,0:T(8,128)(2,1)}, bf16[2,40,2048]{2,1,0:T(8,128)(2,1)S(1)}, u32[]{:S(2)}) copy-start(bf16[2,40,2048]{2,1,0:T(8,128)(2,1)S(1)} %fusion.21) | copy-start | bytes 983044
  295.0 2.8 copy-start
  297.8 30.7 %copy-start.5 = (bf16[16,64,512]{2,1,0:T(8,128)(2,1)S(1)}, bf16[16,64,512]{2,1,0:T(8,128)(2,1)}, u32[]{:S(2)}) copy-start(bf16[16,64,512]{2,1,0:T(8,128)(2,1)} %copy-done.4) | copy-start | bytes 3145732
  328.5 1.6 copy-start.7
Sparse Core Ops, SparseCore 0:
  11.4 93.9 all-gather.1

commit v4 on v3

--- a/solution.py
+++ b/solution.py
@@ -38,13 +38,13 @@
     return moved.reshape(shape)
 
 
-def gather_rows(held, axis):
+def gather_rows(held, axis, dim):
     bit = 1
     while bit < lax.axis_size(axis):
         theirs = exchange(held, axis, bit)
         upper = (lax.axis_index(axis) // bit) % 2 == 1
         held = jnp.concatenate(
-            [jnp.where(upper, theirs, held), jnp.where(upper, held, theirs)], axis=0
+            [jnp.where(upper, theirs, held), jnp.where(upper, held, theirs)], axis=dim
         )
         bit *= 2
     return held
@@ -148,6 +148,11 @@
             pltpu.SemaphoreType.DMA((2 * rounds,)),
             pltpu.SemaphoreType.DMA((2 * rounds,)),
         ],
+        cost_estimate=pl.CostEstimate(
+            flops=2 * count * width * head.shape[1],
+            bytes_accessed=16 * head.size,
+            transcendentals=count * head.shape[1],
+        ),
         compiler_params=pltpu.CompilerParams(
             collective_id=0, has_side_effects=True, vmem_limit_bytes=40 * 2**20
         ),
@@ -187,12 +192,11 @@
     rows = lax.all_gather(
         jnp.concatenate([normed, coded], axis=1), "ep", axis=0, tiled=True
     )
-    gate_full = gather_rows(gate_proj[0], "grp")
-    up_full = gather_rows(up_proj[0], "grp")
-    down_full = gather_rows(down_proj[0], "grp")
-    up_next, gate_full = lax.optimization_barrier((up_proj, gate_full))
-    down_next, up_full = lax.optimization_barrier((down_proj, up_full))
-    spread = tuple(spread_rows(weights) for weights in (gate_proj, up_next, down_next))
+    both_full = gather_rows(jnp.concatenate([gate_proj, up_proj], axis=0), "grp", 1)
+    up_next, both_full = lax.optimization_barrier((up_proj, both_full))
+    down_full = gather_rows(down_proj[0], "grp", 0)
+    gate_full, up_full = both_full[0], both_full[1]
+    spread = (spread_rows(gate_proj), spread_rows(up_next))
     rows, spread = lax.optimization_barrier((rows, spread))
 
     tokens = rows[:, :width]
@@ -203,14 +207,17 @@
     gate_vals = jnp.dot(tokens, gate_full, preferred_element_type=jnp.float32)
     up_vals = jnp.dot(tokens, up_full, preferred_element_type=jnp.float32)
     hidden = (jax.nn.silu(gate_vals) * up_vals).astype(jnp.bfloat16)
+    down_next, hidden = lax.optimization_barrier((down_proj, hidden))
+    down_spread = spread_rows(down_next)
     outputs = jnp.dot(hidden, down_full, preferred_element_type=jnp.float32)
     terms = (outputs * weight[:, None]).reshape(n_ep, -1, width)
     summed = scatter_sum(terms).reshape(states.shape)
     mixed = (residual + summed).astype(jnp.bfloat16)
 
+    down_spread, mixed = lax.optimization_barrier((down_spread, mixed))
     moved = tuple(
         relocate(part, source, weights.shape)
-        for part, weights in zip(spread, (gate_proj, up_proj, down_proj))
+        for part, weights in zip((*spread, down_spread), (gate_proj, up_proj, down_proj))
     )
 
     request_ends = jnp.cumsum(req_lengths[:, 0, :], axis=-1) - 1

time: 342 us -> 312 us (0.912)
  waiting for transfers between devices: 175 us -> 148 us
  Pallas kernels: 30.7 us -> 42.8 us
  matrix products: 19.2 us -> 12.3 us
  starting transfers between devices: 54.5 us -> 47.7 us
    all_to_all x3, waiting for transfers between devices: 34.5 us -> 0.01 us  [relocate(): lax.all_to_all(ordered, 'ep', split_axis=0, concat_axis=0, tiled=True)]
    pallas_call x1, Pallas kernels: 30.7 us -> 42.8 us  [tail_probs(): pl.pallas_call(functools.partial(tail_kernel, ep_bits, grp_bits), out_sha...]
    ppermute x7 -> x6, waiting for transfers between devices: 122 us -> 134 us  [exchange(): return lax.ppermute(value, axis, [(i, i ^ bit) for i in range(n)])]
    dot_general x1, matrix products: 11.4 us -> 2.9 us  [per_device(): outputs = jnp.dot(hidden, down_full, preferred_element_type=jnp.float32)]
    all_to_all x3, starting transfers between devices: 19.7 us -> 14.9 us  [relocate(): lax.all_to_all(ordered, 'ep', split_axis=0, concat_axis=0, tiled=True)]
    all_to_all x3, waiting for transfers between devices: 18.1 us -> 14 us  [spread_rows(): return lax.all_to_all(rows, 'ep', split_axis=0, concat_axis=0, tiled=True)]
    all_to_all x3, starting transfers between devices: 23.5 us -> 19.5 us  [spread_rows(): return lax.all_to_all(rows, 'ep', split_axis=0, concat_axis=0, tiled=True)]
    ppermute x7 -> x6, starting transfers between devices: 11.3 us -> 13.2 us  [exchange(): return lax.ppermute(value, axis, [(i, i ^ bit) for i in range(n)])]
  transfers between devices with their start and end apart: 14 -> 13, of which waited for: 10 -> 7; matrix products, arithmetic and copies ran while one was open for 7% -> 9% of each run, Pallas kernels for 0% -> 14%
where the time goes in v4:
time: 312 us; the launch traced here: 311 us
  waiting for transfers between devices  148 us (47%)
  starting transfers between devices  47.7 us (15%)
  Pallas kernels  42.8 us (14%)
  other arithmetic  24.1 us (8%)
  local copies, waits for them, and re-layouts  22.1 us (7%)
  between operations  14.5 us (5%)
  matrix products  12.3 us (4%)
    ppermute x6, waiting for transfers between devices, exchange(): return lax.ppermute(value, axis, [(i, i ^ bit) for i in range(n)])  134 us
    pallas_call x1, Pallas kernels, tail_probs(): pl.pallas_call(functools.partial(tail_kernel, ep_bits, grp_bits), out_sha...  42.8 us
    all_to_all x3, starting transfers between devices, spread_rows(): return lax.all_to_all(rows, 'ep', split_axis=0, concat_axis=0, tiled=True)  19.5 us
    all_to_all x3, starting transfers between devices, relocate(): lax.all_to_all(ordered, 'ep', split_axis=0, concat_axis=0, tiled=True)  14.9 us
    all_to_all x3, waiting for transfers between devices, spread_rows(): return lax.all_to_all(rows, 'ep', split_axis=0, concat_axis=0, tiled=True)  14 us
    ppermute x6, starting transfers between devices, exchange(): return lax.ppermute(value, axis, [(i, i ^ bit) for i in range(n)])  13.2 us
    unnamed x44, local copies, waits for them, and re-layouts  12.3 us
    add x4, other arithmetic, scatter_sum(): kept + exchange(sent.astype(jnp.bfloat16), 'ep', bit).astype(jnp.float32)  10 us
  transfers between devices with their start and end apart: 13, of which 7 were waited for; matrix products, arithmetic and copies ran while one was open for 9% of the time, Pallas kernels for 14%

profile of v4, /device:TPU:0, one launch (start us, length us, event | category | flops | bytes accessed | tf_op | source)
XLA Modules:
  0.0 311.2 jit_solution(2215833955312683164)
XLA Ops:
  12.8 3.0 collective-permute-start
  15.8 5.9 %all-to-all-start = ((bf16[16,64,512]{2,1,0:T(8,128)(2,1)}), bf16[16,64,512]{2,1,0:T(8,128)(2,1)S(1)}, u32[]{:S(2)}, u32[]{:S(2)}) async-start(bf16[16,64,512]{2,1,0:T(8,128)(2,1)} %bitcast.51), calls=%async_computation | async-start | bytes 2097152 | tf_op jit(solution)/shard_map/all_to_all | solution.py:32
  21.7 39.8 %collective-permute-done = bf16[2,1024,512]{2,1,0:T(8,128)(2,1)} collective-permute-done((bf16[2,1024,512]{2,1,0:T(8,128)(2,1)S(1)}, bf16[2,1024,512]{2,1,0:T(8,128)(2,1)}, u32[]{:S(2)}, u32[]{:S(2)}) %collective-permute-start) | collective-permute-done | bytes 2097184 | tf_op jit(solution)/shard_map/ppermute | solution.py:26
  61.5 1.9 broadcast_select_fusion.1
  63.4 2.3 pad_maximum_fusion
  65.7 6.2 %all-to-all-start.1 = ((bf16[16,64,512]{2,1,0:T(8,128)(2,1)}), bf16[16,64,512]{2,1,0:T(8,128)(2,1)S(1)}, u32[]{:S(2)}, u32[]{:S(2)}) async-start(bf16[16,64,512]{2,1,0:T(8,128)(2,1)} %bitcast.2), calls=%async_computation.1 | async-start | bytes 2097152 | tf_op jit(solution)/shard_map/all_to_all | solution.py:32
  73.6 24.0 %collective-permute-done.1 = bf16[256,2048]{1,0:T(8,128)(2,1)S(1)} collective-permute-done((bf16[256,2048]{1,0:T(8,128)(2,1)}, bf16[256,2048]{1,0:T(8,128)(2,1)S(1)}, u32[]{:S(2)}, u32[]{:S(2)}) %collective-permute-start.1) | collective-permute-done | bytes 1048608 | tf_op jit(solution)/shard_map/ppermute | solution.py:26
  97.6 2.7 broadcast_select_fusion.6
  100.3 3.3 %all-to-all-done.1 = bf16[16,64,512]{2,1,0:T(8,128)(2,1)S(1)} async-done(((bf16[16,64,512]{2,1,0:T(8,128)(2,1)}), bf16[16,64,512]{2,1,0:T(8,128)(2,1)S(1)}, u32[]{:S(2)}, u32[]{:S(2)}) %all-to-all-start.1) | async-done | bytes 1048608 | tf_op jit(solution)/shard_map/all_to_all | solution.py:32
  103.6 5.9 %fusion.2 = f32[1280,512]{1,0:T(8,128)S(1)} fusion(bf16[1280,2176]{1,0:T(8,128)(2,1)} %all-gather.2.cloned.1.call-done, bf16[2,2048,512]{2,1,0:T(8,128)(2,1)} %pad_maximum_fusion), kind=kOutput, calls=%fused_computation.9 | convolution fusion | flops 2684354560 | bytes 9961472 | tf_op jit(solution)/shard_map/dot_general | solution.py:207
  110.0 3.3 %fusion.7 = bf16[1280,512]{1,0:T(8,128)(2,1)S(1)} fusion(bf16[1280,2176]{1,0:T(8,128)(2,1)S(1)} %copy-done.15, f32[1280,512]{1,0:T(8,128)S(1)} %fusion.2, bf16[2,2048,512]{2,1,0:T(8,128)(2,1)S(1)} %copy-done.9), kind=kOutput, calls=%fused_computation.13 | convolution fusion | flops 2688286720 | bytes 11272192 | tf_op jit(solution)/shard_map/dot_general | solution.py:208
  113.5 2.9 convolution_multiply_fusion
  116.4 4.0 %copy-done.3 = f32[1280,2048]{1,0:T(8,128)} copy-done((f32[1280,2048]{1,0:T(8,128)}, f32[1280,2048]{1,0:T(8,128)S(1)}, u32[]{:S(2)}) %copy-start.3) | copy-done | bytes 10485784
  120.4 1.9 fusion.10
  122.4 7.3 %all-to-all-start.2 = ((bf16[16,16,2048]{2,1,0:T(8,128)(2,1)}), bf16[16,16,2048]{2,1,0:T(8,128)(2,1)S(1)}, u32[]{:S(2)}, u32[]{:S(2)}) async-start(bf16[16,16,2048]{2,1,0:T(8,128)(2,1)} %bitcast.5), calls=%async_computation.2 | async-start | bytes 2097152 | tf_op jit(solution)/shard_map/all_to_all | solution.py:32
  129.7 4.1 %bitcast_add_fusion = f32[8,80,2048]{2,1,0:T(8,128)S(1)} fusion(bf16[8,80,2048]{2,1,0:T(8,128)(2,1)} %collective-permute-done.2, f32[8,2,80,2048]{3,2,1,0:T(8,128)} %bitcast.50, s32[]{:T(128)S(6)} %select_n.151), kind=kLoop, calls=%fused_computation.6 | loop fusion | flops 2621440 | bytes 13107204 | tf_op jit(solution)/shard_map/add | solution.py:70
  135.2 1.9 collective-permute-start.3
  138.6 1.8 gather_fusion.3
  142.0 10.7 %all-to-all-done.2 = bf16[16,16,2048]{2,1,0:T(8,128)(2,1)S(1)} async-done(((bf16[16,16,2048]{2,1,0:T(8,128)(2,1)}), bf16[16,16,2048]{2,1,0:T(8,128)(2,1)S(1)}, u32[]{:S(2)}, u32[]{:S(2)}) %all-to-all-start.2) | async-done | bytes 1048608 | tf_op jit(solution)/shard_map/all_to_all | solution.py:32
  152.7 7.0 %all-to-all-start.3 = ((bf16[16,64,512]{2,1,0:T(8,128)(2,1)}), bf16[16,64,512]{2,1,0:T(8,128)(2,1)}, u32[]{:S(2)}, u32[]{:S(2)}) async-start(bf16[16,64,512]{2,1,0:T(8,128)(2,1)} %get-tuple-element.34), calls=%async_computation.3 | async-start | bytes 2097152 | tf_op jit(solution)/shard_map/all_to_all | solution.py:37
  159.7 19.7 %collective-permute-done.3 = bf16[4,80,2048]{2,1,0:T(8,128)(2,1)} collective-permute-done((bf16[4,80,2048]{2,1,0:T(8,128)(2,1)}, bf16[4,80,2048]{2,1,0:T(8,128)(2,1)}, u32[]{:S(2)}, u32[]{:S(2)}) %collective-permute-start.3) | collective-permute-done | bytes 1310752 | tf_op jit(solution)/shard_map/ppermute | solution.py:26
  179.5 2.4 bitcast_add_fusion.1
  182.0 3.7 %collective-permute-start.4 = (bf16[2,80,2048]{2,1,0:T(8,128)(2,1)S(1)}, bf16[2,80,2048]{2,1,0:T(8,128)(2,1)}, u32[]{:S(2)}, u32[]{:S(2)}) collective-permute-start(bf16[2,80,2048]{2,1,0:T(8,128)(2,1)S(1)} %fusion.24), channel_id=1, source_target_pairs={{0,4},{1,5},{2,6},{3,7},{4,0},{5,1},{6,2},{7,3},{8,12},{9,13},{10,... | collective-permute-start | bytes 1966088 | tf_op jit(solution)/shard_map/ppermute | solution.py:26
  185.7 13.5 %collective-permute-done.4 = bf16[2,80,2048]{2,1,0:T(8,128)(2,1)} collective-permute-done((bf16[2,80,2048]{2,1,0:T(8,128)(2,1)S(1)}, bf16[2,80,2048]{2,1,0:T(8,128)(2,1)}, u32[]{:S(2)}, u32[]{:S(2)}) %collective-permute-start.4) | collective-permute-done | bytes 655392 | tf_op jit(solution)/shard_map/ppermute | solution.py:26
  199.2 2.3 bitcast_add_fusion.2
  201.5 4.3 %all-to-all-start.4 = ((bf16[16,64,512]{2,1,0:T(8,128)(2,1)}), bf16[16,64,512]{2,1,0:T(8,128)(2,1)S(1)}, u32[]{:S(2)}, u32[]{:S(2)}) async-start(bf16[16,64,512]{2,1,0:T(8,128)(2,1)} %get-tuple-element.33), calls=%async_computation.4 | async-start | bytes 2097152 | tf_op jit(solution)/shard_map/all_to_all | solution.py:37
  206.9 2.9 collective-permute-start.5
  209.8 36.6 %collective-permute-done.5 = bf16[1,80,2048]{2,1,0:T(8,128)(2,1)S(1)} collective-permute-done((bf16[1,80,2048]{2,1,0:T(8,128)(2,1)S(1)}, bf16[1,80,2048]{2,1,0:T(8,128)(2,1)S(1)}, u32[]{:S(2)}, u32[]{:S(2)}) %collective-permute-start.5) | collective-permute-done | bytes 327712 | tf_op jit(solution)/shard_map/ppermute | solution.py:26
  249.4 3.7 %all-to-all-start.5 = ((bf16[16,16,2048]{2,1,0:T(8,128)(2,1)}), bf16[16,16,2048]{2,1,0:T(8,128)(2,1)S(1)}, u32[]{:S(2)}, u32[]{:S(2)}) async-start(bf16[16,16,2048]{2,1,0:T(8,128)(2,1)} %broadcast_select_fusion.4), calls=%async_computation.5 | async-start | bytes 2097152 | tf_op jit(solution)/shard_map/all_to_all | solution.py:37
  253.9 2.8 copy-done
  256.7 42.8 %shard_map.155 = f32[16,1536]{1,0:T(8,128)S(1)} custom-call(bf16[16,2048]{1,0:T(8,128)(2,1)S(1)} %broadcast_select_fusion.7.tails_ref, f32[1,2048]{1,0:T(1,128)S(1)} %bitcast.44, bf16[2048,1536]{1,0:T(8,128)(2,1)S(1)} %copy-done), custom_call_target="tpu_custom_call" | custom-call | flops 100663296 | bytes 50331648 | tf_op jit(solution)/shard_map/pallas_call | solution.py:138
  299.5 2.3 copy.35
  (89 shorter events, 19.7 us)
Async XLA Ops:
  7.2 4.2 %copy-start.10 = (bf16[1,1024,512]{2,1,0:T(8,128)(2,1)S(1)}, bf16[1,1024,512]{2,1,0:T(8,128)(2,1)}, u32[]{:S(2)}) copy-start(bf16[1,1024,512]{2,1,0:T(8,128)(2,1)} %param.19) | copy-start | bytes 3145732
  7.2 96.4 %all-gather.2.cloned.1.call-start = ((), (), s32[]{:S(2)}) async-start(), calls=%async_computation.6 | async-start | bytes 5918720 | tf_op jit(solution)/shard_map/all_gather | solution.py:192
  12.8 48.7 %collective-permute-start = (bf16[2,1024,512]{2,1,0:T(8,128)(2,1)S(1)}, bf16[2,1024,512]{2,1,0:T(8,128)(2,1)}, u32[]{:S(2)}, u32[]{:S(2)}) collective-permute-start(bf16[2,1024,512]{2,1,0:T(8,128)(2,1)S(1)} %constant_dynamic-update-slice_fusion), channel_id=1, source_target_pairs={{0,16},{16,0},{1,17},{17,1},{2,18},{18,2},{3,19},{19,3},{4,20},{20... | collective-permute-start | bytes 6291464 | tf_op jit(solution)/shard_map/ppermute | solution.py:26
  15.8 49.9 %all-to-all-start = ((bf16[16,64,512]{2,1,0:T(8,128)(2,1)}), bf16[16,64,512]{2,1,0:T(8,128)(2,1)S(1)}, u32[]{:S(2)}, u32[]{:S(2)}) async-start(bf16[16,64,512]{2,1,0:T(8,128)(2,1)} %bitcast.51), calls=%async_computation | async-start | bytes 2097152 | tf_op jit(solution)/shard_map/all_to_all | solution.py:32
  65.7 34.6 %copy-start.6 = (bf16[16,64,512]{2,1,0:T(8,128)(2,1)}, bf16[16,64,512]{2,1,0:T(8,128)(2,1)S(1)}, u32[]{:S(2)}) copy-start(bf16[16,64,512]{2,1,0:T(8,128)(2,1)S(1)} %all-to-all-done) | copy-start | bytes 3145732
  65.7 37.9 %all-to-all-start.1 = ((bf16[16,64,512]{2,1,0:T(8,128)(2,1)}), bf16[16,64,512]{2,1,0:T(8,128)(2,1)S(1)}, u32[]{:S(2)}, u32[]{:S(2)}) async-start(bf16[16,64,512]{2,1,0:T(8,128)(2,1)} %bitcast.2), calls=%async_computation.1 | async-start | bytes 2097152 | tf_op jit(solution)/shard_map/all_to_all | solution.py:32
  71.9 25.7 %collective-permute-start.1 = (bf16[256,2048]{1,0:T(8,128)(2,1)}, bf16[256,2048]{1,0:T(8,128)(2,1)S(1)}, u32[]{:S(2)}, u32[]{:S(2)}) collective-permute-start(bf16[256,2048]{1,0:T(8,128)(2,1)} %bitcast.6), channel_id=1, source_target_pairs={{0,16},{16,0},{1,17},{17,1},{2,18},{18,2},{3,19},{19,3},{4,20},{20... | collective-permute-start | bytes 3145736 | tf_op jit(solution)/shard_map/ppermute | solution.py:26
  103.6 5.9 %copy-start.8 = (bf16[16,64,512]{2,1,0:T(8,128)(2,1)}, bf16[16,64,512]{2,1,0:T(8,128)(2,1)S(1)}, u32[]{:S(2)}) copy-start(bf16[16,64,512]{2,1,0:T(8,128)(2,1)S(1)} %all-to-all-done.1) | copy-start | bytes 3145732
  103.6 5.9 %copy-start.9 = (bf16[2,2048,512]{2,1,0:T(8,128)(2,1)S(1)}, bf16[2,2048,512]{2,1,0:T(8,128)(2,1)}, u32[]{:S(2)}) copy-start(bf16[2,2048,512]{2,1,0:T(8,128)(2,1)} %pad_maximum_fusion) | copy-start | bytes 12582916
  103.6 6.4 %copy-start.15 = (bf16[1280,2176]{1,0:T(8,128)(2,1)S(1)}, bf16[1280,2176]{1,0:T(8,128)(2,1)}, u32[]{:S(2)}) copy-start(bf16[1280,2176]{1,0:T(8,128)(2,1)} %all-gather.2.cloned.1.call-done) | copy-start | bytes 16711684
  110.0 3.5 %copy-start.13 = (bf16[256,2048]{1,0:T(8,128)(2,1)S(1)}, bf16[256,2048]{1,0:T(8,128)(2,1)}, u32[]{:S(2)}) copy-start(bf16[256,2048]{1,0:T(8,128)(2,1)} %get-tuple-element.28) | copy-start | bytes 3145732
  110.0 3.5 %copy-start.14 = (bf16[256,2048]{1,0:T(8,128)(2,1)S(1)}, bf16[256,2048]{1,0:T(8,128)(2,1)}, u32[]{:S(2)}) copy-start(bf16[256,2048]{1,0:T(8,128)(2,1)} %get-tuple-element.29) | copy-start | bytes 3145732
  116.4 4.0 %copy-start.3 = (f32[1280,2048]{1,0:T(8,128)}, f32[1280,2048]{1,0:T(8,128)S(1)}, u32[]{:S(2)}) copy-start(f32[1280,2048]{1,0:T(8,128)S(1)} %convolution_multiply_fusion) | copy-start | bytes 31457284
  122.3 7.5 %collective-permute-start.2 = (bf16[8,80,2048]{2,1,0:T(8,128)(2,1)}, bf16[8,80,2048]{2,1,0:T(8,128)(2,1)}, u32[]{:S(2)}, u32[]{:S(2)}) collective-permute-start(bf16[8,80,2048]{2,1,0:T(8,128)(2,1)} %fusion.10), channel_id=1, source_target_pairs={{0,1},{1,0},{2,3},{3,2},{4,5},{5,4},{6,7},{7,6},{8,9},{9,8},{10,11... | collective-permute-start | bytes 7864328 | tf_op jit(solution)/shard_map/ppermute | solution.py:26
  122.4 30.3 %all-to-all-start.2 = ((bf16[16,16,2048]{2,1,0:T(8,128)(2,1)}), bf16[16,16,2048]{2,1,0:T(8,128)(2,1)S(1)}, u32[]{:S(2)}, u32[]{:S(2)}) async-start(bf16[16,16,2048]{2,1,0:T(8,128)(2,1)} %bitcast.5), calls=%async_computation.2 | async-start | bytes 2097152 | tf_op jit(solution)/shard_map/all_to_all | solution.py:32
  133.9 3.2 %copy-start.2 = (f32[8,80,2048]{2,1,0:T(8,128)}, f32[8,80,2048]{2,1,0:T(8,128)S(1)}, u32[]{:S(2)}) copy-start(f32[8,80,2048]{2,1,0:T(8,128)S(1)} %bitcast_add_fusion) | copy-start | bytes 15728644
  133.9 3.2 %copy-start.18 = (s32[16]{0:T(128)S(1)}, s32[16]{0:T(128)}, u32[]{:S(2)}) copy-start(s32[16]{0:T(128)} %param.23) | copy-start | bytes 196
  133.9 3.2 %copy-start.17 = (s32[16]{0:T(128)S(1)}, s32[16]{0:T(128)}, u32[]{:S(2)}) copy-start(s32[16]{0:T(128)} %param.22) | copy-start | bytes 196
  133.9 4.0 %copy-start.7 = (bf16[16,64,512]{2,1,0:T(8,128)(2,1)S(1)}, bf16[16,64,512]{2,1,0:T(8,128)(2,1)}, u32[]{:S(2)}) copy-start(bf16[16,64,512]{2,1,0:T(8,128)(2,1)} %copy-done.6) | copy-start | bytes 3145732
  135.2 44.3 %collective-permute-start.3 = (bf16[4,80,2048]{2,1,0:T(8,128)(2,1)}, bf16[4,80,2048]{2,1,0:T(8,128)(2,1)}, u32[]{:S(2)}, u32[]{:S(2)}) collective-permute-start(bf16[4,80,2048]{2,1,0:T(8,128)(2,1)} %fusion.18), channel_id=1, source_target_pairs={{0,2},{1,3},{2,0},{3,1},{4,6},{5,7},{6,4},{7,5},{8,10},{9,11},{10,... | collective-permute-start | bytes 3932168 | tf_op jit(solution)/shard_map/ppermute | solution.py:26
  152.7 7.0 %copy-start.4 = (bf16[16,16,2048]{2,1,0:T(8,128)(2,1)}, bf16[16,16,2048]{2,1,0:T(8,128)(2,1)S(1)}, u32[]{:S(2)}) copy-start(bf16[16,16,2048]{2,1,0:T(8,128)(2,1)S(1)} %all-to-all-done.2) | copy-start | bytes 3145732
  152.7 48.8 %all-to-all-start.3 = ((bf16[16,64,512]{2,1,0:T(8,128)(2,1)}), bf16[16,64,512]{2,1,0:T(8,128)(2,1)}, u32[]{:S(2)}, u32[]{:S(2)}) async-start(bf16[16,64,512]{2,1,0:T(8,128)(2,1)} %get-tuple-element.34), calls=%async_computation.3 | async-start | bytes 2097152 | tf_op jit(solution)/shard_map/all_to_all | solution.py:37
  182.0 17.2 %collective-permute-start.4 = (bf16[2,80,2048]{2,1,0:T(8,128)(2,1)S(1)}, bf16[2,80,2048]{2,1,0:T(8,128)(2,1)}, u32[]{:S(2)}, u32[]{:S(2)}) collective-permute-start(bf16[2,80,2048]{2,1,0:T(8,128)(2,1)S(1)} %fusion.24), channel_id=1, source_target_pairs={{0,4},{1,5},{2,6},{3,7},{4,0},{5,1},{6,2},{7,3},{8,12},{9,13},{10,... | collective-permute-start | bytes 1966088 | tf_op jit(solution)/shard_map/ppermute | solution.py:26
  201.5 46.0 %copy-start.11 = (bf16[2,40,2048]{2,1,0:T(8,128)(2,1)S(1)}, bf16[2,40,2048]{2,1,0:T(8,128)(2,1)}, u32[]{:S(2)}) copy-start(bf16[2,40,2048]{2,1,0:T(8,128)(2,1)} %param.14) | copy-start | bytes 983044
  201.5 46.1 %copy-start.5 = (bf16[16,16,2048]{2,1,0:T(8,128)(2,1)S(1)}, bf16[16,16,2048]{2,1,0:T(8,128)(2,1)}, u32[]{:S(2)}) copy-start(bf16[16,16,2048]{2,1,0:T(8,128)(2,1)} %copy-done.4) | copy-start | bytes 3145732
  201.5 47.9 %all-to-all-start.4 = ((bf16[16,64,512]{2,1,0:T(8,128)(2,1)}), bf16[16,64,512]{2,1,0:T(8,128)(2,1)S(1)}, u32[]{:S(2)}, u32[]{:S(2)}) async-start(bf16[16,64,512]{2,1,0:T(8,128)(2,1)} %get-tuple-element.33), calls=%async_computation.4 | async-start | bytes 2097152 | tf_op jit(solution)/shard_map/all_to_all | solution.py:37
  206.9 39.5 %collective-permute-start.5 = (bf16[1,80,2048]{2,1,0:T(8,128)(2,1)S(1)}, bf16[1,80,2048]{2,1,0:T(8,128)(2,1)S(1)}, u32[]{:S(2)}, u32[]{:S(2)}) collective-permute-start(bf16[1,80,2048]{2,1,0:T(8,128)(2,1)S(1)} %dynamic-slice_convert_fusion.2), channel_id=1, source_target_pairs={{0,8},{1,9},{2,10},{3,11},{4,12},{5,13},{6,14},{7,15},{8,0},{9,1},... | collective-permute-start | bytes 983048 | tf_op jit(solution)/shard_map/ppermute | solution.py:26
  247.6 5.9 %copy-start.12 = (bf16[2,40,2048]{2,1,0:T(8,128)(2,1)}, bf16[2,40,2048]{2,1,0:T(8,128)(2,1)S(1)}, u32[]{:S(2)}) copy-start(bf16[2,40,2048]{2,1,0:T(8,128)(2,1)S(1)} %fusion.23) | copy-start | bytes 983044
  248.3 4.9 %copy-start.16 = (s32[2,1,4]{2,1,0:T(1,128)S(1)}, s32[2,1,4]{2,1,0:T(1,128)}, u32[]{:S(2)}) copy-start(s32[2,1,4]{2,1,0:T(1,128)} %param.24) | copy-start | bytes 100
  248.3 5.6 %copy-start.1 = (f32[2048]{0:T(1024)S(1)}, f32[2048]{0:T(1024)}, u32[]{:S(2)}) copy-start(f32[2048]{0:T(1024)} %param.18) | copy-start | bytes 24580
  249.4 50.1 %all-to-all-start.5 = ((bf16[16,16,2048]{2,1,0:T(8,128)(2,1)}), bf16[16,16,2048]{2,1,0:T(8,128)(2,1)S(1)}, u32[]{:S(2)}, u32[]{:S(2)}) async-start(bf16[16,16,2048]{2,1,0:T(8,128)(2,1)} %broadcast_select_fusion.4), calls=%async_computation.5 | async-start | bytes 2097152 | tf_op jit(solution)/shard_map/all_to_all | solution.py:37
  253.9 2.8 copy-start
Sparse Core Ops, SparseCore 0:
  11.5 91.4 all-gather.1

commit v5 on v4

--- a/solution.py
+++ b/solution.py
@@ -214,10 +214,10 @@
     summed = scatter_sum(terms).reshape(states.shape)
     mixed = (residual + summed).astype(jnp.bfloat16)
 
-    down_spread, mixed = lax.optimization_barrier((down_spread, mixed))
+    up_spread, down_spread, mixed = lax.optimization_barrier((spread[1], down_spread, mixed))
     moved = tuple(
         relocate(part, source, weights.shape)
-        for part, weights in zip((*spread, down_spread), (gate_proj, up_proj, down_proj))
+        for part, weights in zip((spread[0], up_spread, down_spread), (gate_proj, up_proj, down_proj))
     )
 
     request_ends = jnp.cumsum(req_lengths[:, 0, :], axis=-1) - 1

time: 312 us -> 342 us (1.096)
  blocking collectives: 0 us -> 28.4 us
  waiting for transfers between devices: 148 us -> 158 us
  starting transfers between devices: 47.7 us -> 38.7 us
    all_to_all x0 -> x1, blocking collectives: none -> 28.4 us  [relocate(): lax.all_to_all(ordered, 'ep', split_axis=0, concat_axis=0, tiled=True)]
    all_to_all x3 -> x2, waiting for transfers between devices: 0.01 us -> 19.9 us  [relocate(): lax.all_to_all(ordered, 'ep', split_axis=0, concat_axis=0, tiled=True)]
    all_to_all x3, waiting for transfers between devices: 14 us -> 3.4 us  [spread_rows(): return lax.all_to_all(rows, 'ep', split_axis=0, concat_axis=0, tiled=True)]
    unnamed x44 -> x46, local copies, waits for them, and re-layouts: 12.3 us -> 16.7 us
    all_to_all x3 -> x2, starting transfers between devices: 14.9 us -> 11.9 us  [relocate(): lax.all_to_all(ordered, 'ep', split_axis=0, concat_axis=0, tiled=True)]
  transfers between devices with their start and end apart: 13 -> 12, of which waited for: 7 -> 8; matrix products, arithmetic and copies ran while one was open for 9% -> 5% of each run, Pallas kernels for 14% -> 13%
where the time goes in v5:
time: 342 us; the launch traced here: 341 us
  waiting for transfers between devices  158 us (46%)
  Pallas kernels  42.8 us (13%)
  starting transfers between devices  38.7 us (11%)
  blocking collectives  28.4 us (8%)
  local copies, waits for them, and re-layouts  24.4 us (7%)
  other arithmetic  21.9 us (6%)
  between operations  14.5 us (4%)
  matrix products  12.3 us (4%)
    ppermute x6, waiting for transfers between devices, exchange(): return lax.ppermute(value, axis, [(i, i ^ bit) for i in range(n)])  134 us
    pallas_call x1, Pallas kernels, tail_probs(): pl.pallas_call(functools.partial(tail_kernel, ep_bits, grp_bits), out_sha...  42.8 us
    all_to_all x1, blocking collectives, relocate(): lax.all_to_all(ordered, 'ep', split_axis=0, concat_axis=0, tiled=True)  28.4 us
    all_to_all x2, waiting for transfers between devices, relocate(): lax.all_to_all(ordered, 'ep', split_axis=0, concat_axis=0, tiled=True)  19.9 us
    unnamed x46, local copies, waits for them, and re-layouts  16.7 us
    all_to_all x3, starting transfers between devices, spread_rows(): return lax.all_to_all(rows, 'ep', split_axis=0, concat_axis=0, tiled=True)  16.5 us
    all_to_all x2, starting transfers between devices, relocate(): lax.all_to_all(ordered, 'ep', split_axis=0, concat_axis=0, tiled=True)  11.9 us
    ppermute x6, starting transfers between devices, exchange(): return lax.ppermute(value, axis, [(i, i ^ bit) for i in range(n)])  10.3 us
  transfers between devices with their start and end apart: 12, of which 8 were waited for; matrix products, arithmetic and copies ran while one was open for 5% of the time, Pallas kernels for 13%

profile of v5, /device:TPU:0, one launch (start us, length us, event | category | flops | bytes accessed | tf_op | source)
XLA Modules:
  0.0 340.7 jit_solution(8575424533927396254)
XLA Ops:
  12.7 3.0 collective-permute-start
  15.7 5.9 %all-to-all-start = ((bf16[16,64,512]{2,1,0:T(8,128)(2,1)}), bf16[16,64,512]{2,1,0:T(8,128)(2,1)S(1)}, u32[]{:S(2)}, u32[]{:S(2)}) async-start(bf16[16,64,512]{2,1,0:T(8,128)(2,1)} %bitcast.53), calls=%async_computation | async-start | bytes 2097152 | tf_op jit(solution)/shard_map/all_to_all | solution.py:32
  21.6 39.8 %collective-permute-done = bf16[2,1024,512]{2,1,0:T(8,128)(2,1)} collective-permute-done((bf16[2,1024,512]{2,1,0:T(8,128)(2,1)S(1)}, bf16[2,1024,512]{2,1,0:T(8,128)(2,1)}, u32[]{:S(2)}, u32[]{:S(2)}) %collective-permute-start) | collective-permute-done | bytes 2097184 | tf_op jit(solution)/shard_map/ppermute | solution.py:26
  61.4 1.9 broadcast_select_fusion.1
  63.3 2.3 pad_maximum_fusion
  65.6 6.2 %all-to-all-start.1 = ((bf16[16,64,512]{2,1,0:T(8,128)(2,1)}), bf16[16,64,512]{2,1,0:T(8,128)(2,1)S(1)}, u32[]{:S(2)}, u32[]{:S(2)}) async-start(bf16[16,64,512]{2,1,0:T(8,128)(2,1)} %bitcast.54), calls=%async_computation.1 | async-start | bytes 2097152 | tf_op jit(solution)/shard_map/all_to_all | solution.py:32
  73.5 24.0 %collective-permute-done.1 = bf16[256,2048]{1,0:T(8,128)(2,1)} collective-permute-done((bf16[256,2048]{1,0:T(8,128)(2,1)S(1)}, bf16[256,2048]{1,0:T(8,128)(2,1)}, u32[]{:S(2)}, u32[]{:S(2)}) %collective-permute-start.1) | collective-permute-done | bytes 1048608 | tf_op jit(solution)/shard_map/ppermute | solution.py:26
  97.5 2.7 broadcast_select_fusion.6
  100.2 3.4 all-to-all-done.1
  103.6 5.9 %fusion.2 = f32[1280,512]{1,0:T(8,128)S(1)} fusion(bf16[1280,2176]{1,0:T(8,128)(2,1)} %all-gather.2.cloned.1.call-done, bf16[2,2048,512]{2,1,0:T(8,128)(2,1)} %pad_maximum_fusion), kind=kOutput, calls=%fused_computation.9 | convolution fusion | flops 2684354560 | bytes 9961472 | tf_op jit(solution)/shard_map/dot_general | solution.py:207
  110.0 3.3 fusion.7
  113.5 2.9 convolution_multiply_fusion
  116.4 4.0 %copy-done.3 = f32[1280,2048]{1,0:T(8,128)} copy-done((f32[1280,2048]{1,0:T(8,128)}, f32[1280,2048]{1,0:T(8,128)S(1)}, u32[]{:S(2)}) %copy-start.3) | copy-done | bytes 10485784
  120.4 2.0 fusion.10
  122.5 5.0 %collective-permute-done.2 = bf16[8,80,2048]{2,1,0:T(8,128)(2,1)S(1)} collective-permute-done((bf16[8,80,2048]{2,1,0:T(8,128)(2,1)}, bf16[8,80,2048]{2,1,0:T(8,128)(2,1)S(1)}, u32[]{:S(2)}, u32[]{:S(2)}) %collective-permute-start.2) | collective-permute-done | bytes 2621472 | tf_op jit(solution)/shard_map/ppermute | solution.py:26
  127.5 3.3 bitcast_add_fusion
  130.8 2.3 copy-done.2
  133.3 2.3 collective-permute-start.3
  135.6 29.4 %collective-permute-done.3 = bf16[4,80,2048]{2,1,0:T(8,128)(2,1)} collective-permute-done((bf16[4,80,2048]{2,1,0:T(8,128)(2,1)S(1)}, bf16[4,80,2048]{2,1,0:T(8,128)(2,1)}, u32[]{:S(2)}, u32[]{:S(2)}) %collective-permute-start.3) | collective-permute-done | bytes 1310752 | tf_op jit(solution)/shard_map/ppermute | solution.py:26
  164.9 2.4 bitcast_add_fusion.1
  167.5 3.3 collective-permute-start.4
  171.6 4.4 %all-to-all-start.2 = ((bf16[16,16,2048]{2,1,0:T(8,128)(2,1)}), bf16[16,16,2048]{2,1,0:T(8,128)(2,1)}, u32[]{:S(2)}, u32[]{:S(2)}) async-start(bf16[16,16,2048]{2,1,0:T(8,128)(2,1)} %bitcast.51), calls=%async_computation.2 | async-start | bytes 2097152 | tf_op jit(solution)/shard_map/all_to_all | solution.py:32
  175.9 20.3 %collective-permute-done.4 = bf16[2,80,2048]{2,1,0:T(8,128)(2,1)} collective-permute-done((bf16[2,80,2048]{2,1,0:T(8,128)(2,1)S(1)}, bf16[2,80,2048]{2,1,0:T(8,128)(2,1)}, u32[]{:S(2)}, u32[]{:S(2)}) %collective-permute-start.4) | collective-permute-done | bytes 655392 | tf_op jit(solution)/shard_map/ppermute | solution.py:26
  200.4 16.0 %collective-permute-done.5 = bf16[1,80,2048]{2,1,0:T(8,128)(2,1)S(1)} collective-permute-done((bf16[1,80,2048]{2,1,0:T(8,128)(2,1)S(1)}, bf16[1,80,2048]{2,1,0:T(8,128)(2,1)S(1)}, u32[]{:S(2)}, u32[]{:S(2)}) %collective-permute-start.5) | collective-permute-done | bytes 327712 | tf_op jit(solution)/shard_map/ppermute | solution.py:26
  219.5 28.4 %all_to_all.30 = bf16[16,64,512]{2,1,0:T(8,128)(2,1)S(1)} all-to-all(bf16[16,64,512]{2,1,0:T(8,128)(2,1)S(1)} %get-tuple-element.36), channel_id=1, replica_groups=mesh['grp'=2,'ep'=16] {'ep'}, dimensions={0} | all-to-all | bytes 2097152 | tf_op jit(solution)/shard_map/all_to_all | solution.py:37
  247.8 5.0 %all-to-all-start.4 = ((bf16[16,64,512]{2,1,0:T(8,128)(2,1)}), bf16[16,64,512]{2,1,0:T(8,128)(2,1)S(1)}, u32[]{:S(2)}, u32[]{:S(2)}) async-start(bf16[16,64,512]{2,1,0:T(8,128)(2,1)} %get-tuple-element.35), calls=%async_computation.4 | async-start | bytes 2097152 | tf_op jit(solution)/shard_map/all_to_all | solution.py:37
  252.8 1.8 gather_fusion.1
  255.8 19.9 %all-to-all-done.4 = bf16[16,64,512]{2,1,0:T(8,128)(2,1)S(1)} async-done(((bf16[16,64,512]{2,1,0:T(8,128)(2,1)}), bf16[16,64,512]{2,1,0:T(8,128)(2,1)S(1)}, u32[]{:S(2)}, u32[]{:S(2)}) %all-to-all-start.4) | async-done | bytes 1048608 | tf_op jit(solution)/shard_map/all_to_all | solution.py:37
  275.8 6.9 %all-to-all-start.5 = ((bf16[16,16,2048]{2,1,0:T(8,128)(2,1)}), bf16[16,16,2048]{2,1,0:T(8,128)(2,1)}, u32[]{:S(2)}, u32[]{:S(2)}) async-start(bf16[16,16,2048]{2,1,0:T(8,128)(2,1)} %broadcast_select_fusion.4), calls=%async_computation.5 | async-start | bytes 2097152 | tf_op jit(solution)/shard_map/all_to_all | solution.py:37
  283.4 2.8 copy-done
  286.2 42.8 %shard_map.155 = f32[16,1536]{1,0:T(8,128)S(1)} custom-call(bf16[16,2048]{1,0:T(8,128)(2,1)S(1)} %broadcast_select_fusion.7.tails_ref, f32[1,2048]{1,0:T(1,128)S(1)} %bitcast.44, bf16[2048,1536]{1,0:T(8,128)(2,1)S(1)} %copy-done), custom_call_target="tpu_custom_call" | custom-call | flops 100663296 | bytes 50331648 | tf_op jit(solution)/shard_map/pallas_call | solution.py:138
  330.9 2.3 copy.37
  (90 shorter events, 20.5 us)
Async XLA Ops:
  7.2 4.2 %copy-start.9 = (bf16[1,1024,512]{2,1,0:T(8,128)(2,1)S(1)}, bf16[1,1024,512]{2,1,0:T(8,128)(2,1)}, u32[]{:S(2)}) copy-start(bf16[1,1024,512]{2,1,0:T(8,128)(2,1)} %param.19) | copy-start | bytes 3145732
  7.2 96.4 %all-gather.2.cloned.1.call-start = ((), (), s32[]{:S(2)}) async-start(), calls=%async_computation.6 | async-start | bytes 5918720 | tf_op jit(solution)/shard_map/all_gather | solution.py:192
  11.4 1.2 copy-start.10
  12.7 48.7 %collective-permute-start = (bf16[2,1024,512]{2,1,0:T(8,128)(2,1)S(1)}, bf16[2,1024,512]{2,1,0:T(8,128)(2,1)}, u32[]{:S(2)}, u32[]{:S(2)}) collective-permute-start(bf16[2,1024,512]{2,1,0:T(8,128)(2,1)S(1)} %constant_dynamic-update-slice_fusion), channel_id=1, source_target_pairs={{0,16},{16,0},{1,17},{17,1},{2,18},{18,2},{3,19},{19,3},{4,20},{20... | collective-permute-start | bytes 6291464 | tf_op jit(solution)/shard_map/ppermute | solution.py:26
  15.7 49.9 %all-to-all-start = ((bf16[16,64,512]{2,1,0:T(8,128)(2,1)}), bf16[16,64,512]{2,1,0:T(8,128)(2,1)S(1)}, u32[]{:S(2)}, u32[]{:S(2)}) async-start(bf16[16,64,512]{2,1,0:T(8,128)(2,1)} %bitcast.53), calls=%async_computation | async-start | bytes 2097152 | tf_op jit(solution)/shard_map/all_to_all | solution.py:32
  63.3 8.6 %copy-start.4 = (bf16[1,256,2048]{2,1,0:T(8,128)(2,1)S(1)}, bf16[1,256,2048]{2,1,0:T(8,128)(2,1)}, u32[]{:S(2)}) copy-start(bf16[1,256,2048]{2,1,0:T(8,128)(2,1)} %param.21) | copy-start | bytes 3145732
  65.6 34.6 %copy-start.5 = (bf16[16,64,512]{2,1,0:T(8,128)(2,1)}, bf16[16,64,512]{2,1,0:T(8,128)(2,1)S(1)}, u32[]{:S(2)}) copy-start(bf16[16,64,512]{2,1,0:T(8,128)(2,1)S(1)} %all-to-all-done) | copy-start | bytes 3145732
  65.6 38.0 %all-to-all-start.1 = ((bf16[16,64,512]{2,1,0:T(8,128)(2,1)}), bf16[16,64,512]{2,1,0:T(8,128)(2,1)S(1)}, u32[]{:S(2)}, u32[]{:S(2)}) async-start(bf16[16,64,512]{2,1,0:T(8,128)(2,1)} %bitcast.54), calls=%async_computation.1 | async-start | bytes 2097152 | tf_op jit(solution)/shard_map/all_to_all | solution.py:32
  71.9 25.7 %collective-permute-start.1 = (bf16[256,2048]{1,0:T(8,128)(2,1)S(1)}, bf16[256,2048]{1,0:T(8,128)(2,1)}, u32[]{:S(2)}, u32[]{:S(2)}) collective-permute-start(bf16[256,2048]{1,0:T(8,128)(2,1)S(1)} %bitcast.52), channel_id=1, source_target_pairs={{0,16},{16,0},{1,17},{17,1},{2,18},{18,2},{3,19},{19,3},{4,20},{20... | collective-permute-start | bytes 3145736 | tf_op jit(solution)/shard_map/ppermute | solution.py:26
  103.6 6.0 %copy-start.6 = (bf16[16,64,512]{2,1,0:T(8,128)(2,1)}, bf16[16,64,512]{2,1,0:T(8,128)(2,1)S(1)}, u32[]{:S(2)}) copy-start(bf16[16,64,512]{2,1,0:T(8,128)(2,1)S(1)} %all-to-all-done.1) | copy-start | bytes 3145732
  103.6 6.0 %copy-start.8 = (bf16[2,2048,512]{2,1,0:T(8,128)(2,1)S(1)}, bf16[2,2048,512]{2,1,0:T(8,128)(2,1)}, u32[]{:S(2)}) copy-start(bf16[2,2048,512]{2,1,0:T(8,128)(2,1)} %pad_maximum_fusion) | copy-start | bytes 12582916
  103.6 6.4 %copy-start.16 = (bf16[1280,2176]{1,0:T(8,128)(2,1)S(1)}, bf16[1280,2176]{1,0:T(8,128)(2,1)}, u32[]{:S(2)}) copy-start(bf16[1280,2176]{1,0:T(8,128)(2,1)} %all-gather.2.cloned.1.call-done) | copy-start | bytes 16711684
  110.0 3.5 %copy-start.14 = (bf16[256,2048]{1,0:T(8,128)(2,1)S(1)}, bf16[256,2048]{1,0:T(8,128)(2,1)}, u32[]{:S(2)}) copy-start(bf16[256,2048]{1,0:T(8,128)(2,1)} %get-tuple-element.30) | copy-start | bytes 3145732
  110.0 3.5 %copy-start.15 = (bf16[256,2048]{1,0:T(8,128)(2,1)S(1)}, bf16[256,2048]{1,0:T(8,128)(2,1)}, u32[]{:S(2)}) copy-start(bf16[256,2048]{1,0:T(8,128)(2,1)} %get-tuple-element.31) | copy-start | bytes 3145732
  116.4 4.0 %copy-start.3 = (f32[1280,2048]{1,0:T(8,128)}, f32[1280,2048]{1,0:T(8,128)S(1)}, u32[]{:S(2)}) copy-start(f32[1280,2048]{1,0:T(8,128)S(1)} %convolution_multiply_fusion) | copy-start | bytes 31457284
  122.4 5.1 %collective-permute-start.2 = (bf16[8,80,2048]{2,1,0:T(8,128)(2,1)}, bf16[8,80,2048]{2,1,0:T(8,128)(2,1)S(1)}, u32[]{:S(2)}, u32[]{:S(2)}) collective-permute-start(bf16[8,80,2048]{2,1,0:T(8,128)(2,1)} %fusion.10), channel_id=1, source_target_pairs={{0,1},{1,0},{2,3},{3,2},{4,5},{5,4},{6,7},{7,6},{8,9},{9,8},{10,11... | collective-permute-start | bytes 7864328 | tf_op jit(solution)/shard_map/ppermute | solution.py:26
  130.8 2.3 copy-start.2
  133.3 31.6 %collective-permute-start.3 = (bf16[4,80,2048]{2,1,0:T(8,128)(2,1)S(1)}, bf16[4,80,2048]{2,1,0:T(8,128)(2,1)}, u32[]{:S(2)}, u32[]{:S(2)}) collective-permute-start(bf16[4,80,2048]{2,1,0:T(8,128)(2,1)S(1)} %fusion.18), channel_id=1, source_target_pairs={{0,2},{1,3},{2,0},{3,1},{4,6},{5,7},{6,4},{7,5},{8,10},{9,11},{10,... | collective-permute-start | bytes 3932168 | tf_op jit(solution)/shard_map/ppermute | solution.py:26
  135.6 35.2 %copy-start.19 = (s32[16]{0:T(128)S(1)}, s32[16]{0:T(128)}, u32[]{:S(2)}) copy-start(s32[16]{0:T(128)} %param.23) | copy-start | bytes 196
  135.6 35.2 %copy-start.18 = (s32[16]{0:T(128)S(1)}, s32[16]{0:T(128)}, u32[]{:S(2)}) copy-start(s32[16]{0:T(128)} %param.22) | copy-start | bytes 196
  167.5 28.7 %collective-permute-start.4 = (bf16[2,80,2048]{2,1,0:T(8,128)(2,1)S(1)}, bf16[2,80,2048]{2,1,0:T(8,128)(2,1)}, u32[]{:S(2)}, u32[]{:S(2)}) collective-permute-start(bf16[2,80,2048]{2,1,0:T(8,128)(2,1)S(1)} %fusion.24), channel_id=1, source_target_pairs={{0,4},{1,5},{2,6},{3,7},{4,0},{5,1},{6,2},{7,3},{8,12},{9,13},{10,... | collective-permute-start | bytes 1966088 | tf_op jit(solution)/shard_map/ppermute | solution.py:26
  171.6 46.1 %all-to-all-start.2 = ((bf16[16,16,2048]{2,1,0:T(8,128)(2,1)}), bf16[16,16,2048]{2,1,0:T(8,128)(2,1)}, u32[]{:S(2)}, u32[]{:S(2)}) async-start(bf16[16,16,2048]{2,1,0:T(8,128)(2,1)} %bitcast.51), calls=%async_computation.2 | async-start | bytes 2097152 | tf_op jit(solution)/shard_map/all_to_all | solution.py:32
  197.4 1.1 copy-start.11
  197.5 20.1 %copy-start.12 = (bf16[2,40,2048]{2,1,0:T(8,128)(2,1)S(1)}, bf16[2,40,2048]{2,1,0:T(8,128)(2,1)}, u32[]{:S(2)}) copy-start(bf16[2,40,2048]{2,1,0:T(8,128)(2,1)} %param.14) | copy-start | bytes 983044
  197.5 20.1 %copy-start.7 = (bf16[16,64,512]{2,1,0:T(8,128)(2,1)S(1)}, bf16[16,64,512]{2,1,0:T(8,128)(2,1)}, u32[]{:S(2)}) copy-start(bf16[16,64,512]{2,1,0:T(8,128)(2,1)} %copy-done.6) | copy-start | bytes 3145732
  197.5 18.8 %collective-permute-start.5 = (bf16[1,80,2048]{2,1,0:T(8,128)(2,1)S(1)}, bf16[1,80,2048]{2,1,0:T(8,128)(2,1)S(1)}, u32[]{:S(2)}, u32[]{:S(2)}) collective-permute-start(bf16[1,80,2048]{2,1,0:T(8,128)(2,1)S(1)} %dynamic-slice_convert_fusion.2), channel_id=1, source_target_pairs={{0,8},{1,9},{2,10},{3,11},{4,12},{5,13},{6,14},{7,15},{8,0},{9,1},... | collective-permute-start | bytes 983048 | tf_op jit(solution)/shard_map/ppermute | solution.py:26
  217.6 65.5 %copy-start.13 = (bf16[2,40,2048]{2,1,0:T(8,128)(2,1)}, bf16[2,40,2048]{2,1,0:T(8,128)(2,1)S(1)}, u32[]{:S(2)}) copy-start(bf16[2,40,2048]{2,1,0:T(8,128)(2,1)S(1)} %fusion.23) | copy-start | bytes 983044
  247.8 27.9 %all-to-all-start.4 = ((bf16[16,64,512]{2,1,0:T(8,128)(2,1)}), bf16[16,64,512]{2,1,0:T(8,128)(2,1)S(1)}, u32[]{:S(2)}, u32[]{:S(2)}) async-start(bf16[16,64,512]{2,1,0:T(8,128)(2,1)} %get-tuple-element.35), calls=%async_computation.4 | async-start | bytes 2097152 | tf_op jit(solution)/shard_map/all_to_all | solution.py:37
  254.7 28.0 %copy-start.17 = (s32[2,1,4]{2,1,0:T(1,128)S(1)}, s32[2,1,4]{2,1,0:T(1,128)}, u32[]{:S(2)}) copy-start(s32[2,1,4]{2,1,0:T(1,128)} %param.24) | copy-start | bytes 100
  254.7 28.7 %copy-start.1 = (f32[2048]{0:T(1024)S(1)}, f32[2048]{0:T(1024)}, u32[]{:S(2)}) copy-start(f32[2048]{0:T(1024)} %param.18) | copy-start | bytes 24580
  275.8 53.2 %all-to-all-start.5 = ((bf16[16,16,2048]{2,1,0:T(8,128)(2,1)}), bf16[16,16,2048]{2,1,0:T(8,128)(2,1)}, u32[]{:S(2)}, u32[]{:S(2)}) async-start(bf16[16,16,2048]{2,1,0:T(8,128)(2,1)} %broadcast_select_fusion.4), calls=%async_computation.5 | async-start | bytes 2097152 | tf_op jit(solution)/shard_map/all_to_all | solution.py:37
  283.4 2.8 copy-start
Sparse Core Ops, SparseCore 0:
  11.5 91.3 all-gather.1
